TPU v7x, 256 devices: a whole 4x4x8 slice. The times are simulated.
256 devices in a mesh: blk: 16 (over z, core), uly: 16 (over y, x).
Axes of the slice: x: 4, y: 4, z: 8, core: 2. Of those that a mesh axis runs over, the one named last changes fastest.
Arguments:
- query: bfloat16 [2048, 6144], P('blk', 'uly'), may hold values from -21 to 21
- key: bfloat16 [2048, 6144], P('blk', 'uly'), may hold values from -3 to 3
- value: bfloat16 [2048, 6144], P('blk', 'uly'), may hold values from -6 to 6
- grad_out: bfloat16 [2048, 6144], P('blk', 'uly'), may hold values from -6 to 6
- tile_mask: int32 [48, 16, 16], replicated, may hold values from 0 to 1, as said below
- tile_order: int32 [16], replicated, may hold values from 0 to 15, each once
Outputs:
- grad_query: bfloat16 [2048, 6144], P(('blk', 'uly'))
- grad_key: bfloat16 [2048, 6144], P(('blk', 'uly'))
- grad_value: bfloat16 [2048, 6144], P(('blk', 'uly'))
Inputs may be any that keep to these rules, and one draw needn't show every extreme that they name: `tile_mask`: every head keeps the diagonal tiles (a tile with itself); rows of tiles keep different shares.
All inputs are finite; a program needn't handle non-finite values.
Results may differ from a plain program's by a relative error of at most 0.007.
Values may be sent and summed in bfloat16 or wider, within the bound.
A program may use at most 64 MiB of HBM per device.

v0:
```python
import jax
import jax.numpy as jnp
from jax import lax
from jax.sharding import PartitionSpec as P

H = 48
DH = 128
TILE = 128


def expand_tiles(tiles):
    groups, first, second = tiles.shape
    large = jnp.broadcast_to(tiles[:, :, None, :, None] > 0, (groups, first, TILE, second, TILE))
    return large.reshape(groups, first * TILE, second * TILE)


def scaled_scores(left, right):
    return jnp.einsum("qhd,khd->hqk", left, right, preferred_element_type=jnp.float32) * DH ** (
        -0.5
    )


def local(query, key, value, grad_out, tile_mask, tile_order):
    factor = DH ** (-0.5)
    heads = H // lax.axis_size("uly")
    q_local, k_local, v_local, g_local = (query, key, value, grad_out)
    rows = q_local.shape[0]
    q_heads = q_local.reshape(rows, heads, DH)
    k_heads = k_local.reshape(rows, heads, DH)
    v_heads = v_local.reshape(rows, heads, DH)
    g_heads = g_local.reshape(rows, heads, DH)
    k_gathered, v_gathered = (
        lax.all_gather(k_local, "blk", axis=0, tiled=True),
        lax.all_gather(v_local, "blk", axis=0, tiled=True),
    )
    total = k_gathered.shape[0]
    k_every = k_gathered.reshape(total, heads, DH)
    v_every = v_gathered.reshape(total, heads, DH)
    head_start = lax.axis_index("uly") * heads
    row_start = lax.axis_index("blk") * rows
    head_mask = lax.dynamic_slice_in_dim(tile_mask, head_start, heads, 0)
    head_mask = jnp.take(jnp.take(head_mask, tile_order, axis=1), tile_order, axis=2)
    local_mask = lax.dynamic_slice_in_dim(head_mask, row_start // TILE, rows // TILE, 1)
    width = min(total, 512)
    steps_count = total // width

    def block_inputs(index):
        start = index * width
        k_block = lax.dynamic_slice_in_dim(k_every, start, width, 0)
        v_block = lax.dynamic_slice_in_dim(v_every, start, width, 0)
        tiles = lax.dynamic_slice_in_dim(local_mask, start // TILE, width // TILE, 2)
        return (k_block, v_block, tiles)

    def stats_step(index, carry):
        k_block, v_block, tiles = block_inputs(index)
        largest, summed = carry
        allowed = expand_tiles(tiles)
        scores = scaled_scores(q_heads, k_block)
        block_max = jnp.max(jnp.where(allowed, scores, -1e30), axis=2)
        new_max = jnp.maximum(largest, block_max)
        added = jnp.sum(jnp.where(allowed, jnp.exp(scores - new_max[:, :, None]), 0.0), axis=2)
        return (new_max, summed * jnp.exp(largest - new_max) + added)

    start_max = jnp.full((heads, rows), -1e30, jnp.float32)
    start_sum = jnp.zeros((heads, rows), jnp.float32)
    largest, summed = lax.fori_loop(0, steps_count, stats_step, (start_max, start_sum))
    lse = largest + jnp.log(summed)

    def output_step(index, accum):
        k_block, v_block, tiles = block_inputs(index)
        allowed = expand_tiles(tiles)
        prob = jnp.where(allowed, jnp.exp(scaled_scores(q_heads, k_block) - lse[:, :, None]), 0.0)
        return accum + jnp.einsum(
            "hqk,khd->qhd", prob.astype(jnp.bfloat16), v_block, preferred_element_type=jnp.float32
        )

    output = lax.fori_loop(0, steps_count, output_step, jnp.zeros((rows, heads, DH), jnp.float32))
    delta = jnp.sum(g_heads.astype(jnp.float32) * output, axis=2).T

    def query_step(index, accum):
        k_block, v_block, tiles = block_inputs(index)
        allowed = expand_tiles(tiles)
        prob = jnp.where(allowed, jnp.exp(scaled_scores(q_heads, k_block) - lse[:, :, None]), 0.0)
        dprob = jnp.einsum("qhd,khd->hqk", g_heads, v_block, preferred_element_type=jnp.float32)
        dscore = (prob * (dprob - delta[:, :, None]) * factor).astype(jnp.bfloat16)
        return accum + jnp.einsum(
            "hqk,khd->qhd", dscore, k_block, preferred_element_type=jnp.float32
        )

    grad_q = lax.fori_loop(0, steps_count, query_step, jnp.zeros((rows, heads, DH), jnp.float32))
    key_mask = lax.dynamic_slice_in_dim(head_mask, row_start // TILE, rows // TILE, 2)
    lse_all, delta_all = (
        lax.all_gather(lse.T, "blk", axis=0, tiled=True),
        lax.all_gather(delta.T, "blk", axis=0, tiled=True),
    )
    empty = jnp.zeros((rows, heads, DH), jnp.float32)
    carry = (empty, empty)
    q_piece = lax.all_gather(q_local, "blk", axis=0, tiled=True)
    g_piece = lax.all_gather(g_local, "blk", axis=0, tiled=True)
    count = q_piece.shape[0]
    q_rows = q_piece.reshape(count, heads, DH)
    g_rows = g_piece.reshape(count, heads, DH)
    tile_rows = jnp.arange(count, dtype=jnp.int32) // TILE
    row_mask = jnp.take(key_mask, tile_rows, axis=1)
    allowed = jnp.broadcast_to(
        row_mask[:, :, :, None] > 0, (heads, count, rows // TILE, TILE)
    ).reshape(heads, count, rows)
    prob = jnp.where(allowed, jnp.exp(scaled_scores(q_rows, k_heads) - lse_all.T[:, :, None]), 0.0)
    dprob = jnp.einsum("qhd,khd->hqk", g_rows, v_heads, preferred_element_type=jnp.float32)
    dscore = (prob * (dprob - delta_all.T[:, :, None]) * factor).astype(jnp.bfloat16)
    key_acc = jnp.einsum("hqk,qhd->khd", dscore, q_rows, preferred_element_type=jnp.float32)
    value_acc = jnp.einsum(
        "hqk,qhd->khd", prob.astype(jnp.bfloat16), g_rows, preferred_element_type=jnp.float32
    )
    key_acc, value_acc = (key_acc, value_acc)
    grad_k = key_acc.reshape(rows, heads * DH)
    grad_v = value_acc.reshape(rows, heads * DH)
    grad_q_b = grad_q.reshape(rows, heads * DH).astype(jnp.bfloat16)
    grad_k_b = grad_k.astype(jnp.bfloat16)
    grad_v_b = grad_v.astype(jnp.bfloat16)
    final_q, final_k, final_v = (
        lax.all_to_all(grad_q_b, "uly", split_axis=0, concat_axis=1, tiled=True),
        lax.all_to_all(grad_k_b, "uly", split_axis=0, concat_axis=1, tiled=True),
        lax.all_to_all(grad_v_b, "uly", split_axis=0, concat_axis=1, tiled=True),
    )
    return (final_q, final_k, final_v)


def solution(mesh):
    placed = (P("blk", "uly"), P("blk", "uly"), P("blk", "uly"), P("blk", "uly"), P(), P())
    return jax.shard_map(
        local,
        mesh=mesh,
        in_specs=placed,
        out_specs=(P(("blk", "uly"), None), P(("blk", "uly"), None), P(("blk", "uly"), None)),
        check_vma=False,
    )
```

profile of v0, /device:TPU:1, one launch (start us, length us, event | category | flops | bytes accessed | tf_op | source)
XLA Modules:
  0.0 212.7 jit_solution(15701123206756458015)
XLA Ops:
  7.2 1.7 copy.85
  9.0 1.6 copy.92
  10.7 1.6 copy.88
  12.4 1.6 copy.93
  19.5 5.5 %gather_fusion.2 = s32[2048,3]{1,0:T(8,128)S(1)} fusion(s32[3,16]{0,1:T(8,128)S(1)} %copy.103, s32[2048]{0:T(1024)S(1)} %broadcast_clamp_fusion), kind=kCustom, calls=%fused_computation.2 | custom fusion | bytes 57344 | tf_op jit(solution)/shard_map/jit(_take)/gather | solution.py:104
  25.7 28.1 %all-gather.5.cloned.1.call-done = bf16[2048,384]{0,1:T(8,128)(2,1)} async-done(((bf16[128,384]{0,1:T(8,128)(2,1)}), bf16[2048,384]{0,1:T(8,128)(2,1)}) %all-gather.5.cloned.1.call-update) | async-done | bytes 1572880 | tf_op jit(solution)/shard_map/all_gather | solution.py:33
  53.7 1.9 copy.97
  55.6 4.2 %while.50 = (s32[]{:T(128)}, f32[3,128]{1,0:T(4,128)S(1)}, f32[3,128]{1,0:T(4,128)S(1)}, s32[3,1,16]{2,0,1:T(4,128)S(1)}, bf16[2048,3,128]{2,0,1:T(8,128)(2,1)S(...) while((s32[]{:T(128)}, f32[3,128]{1,0:T(4,128)S(1)}, ...), condition=%wide.region_3.4_spmd.clone, body=%wide.region_0.3_spmd.clone.sunk | while | flops 51513248 | bytes 2092997 | solution.py:66
  59.9 34.5 %all-gather.7.cloned.1.call-done = bf16[2048,384]{0,1:T(8,128)(2,1)} async-done(((bf16[128,384]{0,1:T(8,128)(2,1)}), bf16[2048,384]{0,1:T(8,128)(2,1)}) %all-gather.7.cloned.1.call-update) | async-done | bytes 1572880 | tf_op jit(solution)/shard_map/all_gather | solution.py:34
  94.4 7.0 %while.51 = (s32[]{:T(128)}, f32[128,3,128]{0,2,1:T(8,128)S(1)}, bf16[2048,3,128]{0,2,1:T(8,128)(2,1)}, s32[3,1,16]{2,0,1:T(4,128)S(1)}, bf16[2048,3,128]{2,0,1:...) while((s32[]{:T(128)}, f32[128,3,128]{0,2,1:T(8,128)S(1)}, ...), condition=%wide.region_5.6_spmd.clone, body=%wide.region_4.5_spmd.clone.sunk | while | flops 101548064 | bytes 1288647 | solution.py:77
  94.6 1.5 fusion.95
  101.5 8.5 %while.52 = (s32[]{:T(128)}, f32[128,3,128]{0,2,1:T(8,128)S(1)}, bf16[2048,3,128]{2,0,1:T(8,128)(2,1)S(1)}, s32[3,1,16]{2,0,1:T(4,128)S(1)}, bf16[128,3,128]{2,0...) while((s32[]{:T(128)}, f32[128,3,128]{0,2,1:T(8,128)S(1)}, ...), condition=%wide.region_8.9_spmd.clone, body=%wide.region_7.8_spmd.clone.sunk | while | flops 152469536 | bytes 3355099 | solution.py:90
  106.3 1.6 fusion.103
  110.8 6.7 %all-to-all-start = ((bf16[16,8,384]{2,1,0:T(8,128)(2,1)}), bf16[16,8,384]{2,1,0:T(8,128)(2,1)}, u32[]{:S(2)}, u32[]{:S(2)}) async-start(bf16[16,8,384]{2,1,0:T(8,128)(2,1)} %convert_element_type.56), calls=%async_computation | async-start | bytes 196608 | tf_op jit(solution)/shard_map/all_to_all | solution.py:122
  117.6 17.1 %all_gather.23 = f32[2048,3]{0,1:T(4,128)S(1)} all-gather(f32[128,3]{0,1:T(4,128)S(1)} %bitcast.120), channel_id=1, replica_groups=mesh['blk'=16,'uly'=16] {'blk'}, dimensions={0}, use_global_device_ids=true | all-gather | bytes 26112 | tf_op jit(solution)/shard_map/all_gather | solution.py:94
  134.7 14.5 %all_gather.21 = f32[2048,3]{0,1:T(4,128)S(1)} all-gather(f32[128,3]{0,1:T(4,128)S(1)} %bitcast.125), channel_id=1, replica_groups=mesh['blk'=16,'uly'=16] {'blk'}, dimensions={0}, use_global_device_ids=true | all-gather | bytes 26112 | tf_op jit(solution)/shard_map/all_gather | solution.py:93
  149.2 5.6 %exponential_select_fusion = f32[3,2048,128]{2,1,0:T(8,128)S(1)} fusion(bf16[2048,3,128]{0,2,1:T(8,128)(2,1)} %bitcast.109, bf16[128,3,128]{0,2,1:T(8,128)(2,1)S(1)} %bitcast.115, f32[3,2048]{1,0:T(4,128)S(1)} %bitcast.123, pred[3,2048]{1,0:T(4,128)(4,1)S(1)} %copy.104), kind=kOutput, calls=%fused_computation.60 | convolution fusion | flops 203685888 | bytes 4847616 | tf_op jit(solution)/shard_map/qhd,khd->hqk/dot_general | solution.py:18
  154.8 20.3 %all-gather.11.cloned.1.call-done = bf16[2048,384]{0,1:T(8,128)(2,1)} async-done(((bf16[128,384]{0,1:T(8,128)(2,1)}), bf16[2048,384]{0,1:T(8,128)(2,1)}) %all-gather.11.cloned.1.call-update) | async-done | bytes 1572880 | tf_op jit(solution)/shard_map/all_gather | solution.py:99
  175.1 4.0 %fusion.53 = bf16[128,3,128]{2,0,1:T(8,128)(2,1)S(1)} fusion(bf16[2048,3,128]{0,2,1:T(8,128)(2,1)} %bitcast.110, f32[3,2048,128]{2,1,0:T(8,128)S(1)} %exponential_select_fusion, bf16[2048,3,128]{0,2,1:T(8,128)(2,1)} %bitcast.103, bf16[128,3,128]{0,2,1:T(8,128)(2,1)S(1)} %bitcast.112, f32[3,2048]{1,0:T(4,128)S(1)} %bitcast.118), kind=kOutput, calls=%fused_computation.67 | convolution fusion | flops 405848064 | bytes 6512640 | tf_op jit(solution)/shard_map/hqk,qhd->khd/dot_general | solution.py:111
  179.9 6.6 %all-to-all-start.1 = ((bf16[16,8,384]{2,1,0:T(8,128)(2,1)}), bf16[16,8,384]{2,1,0:T(8,128)(2,1)S(1)}, u32[]{:S(2)}, u32[]{:S(2)}) async-start(bf16[16,8,384]{2,1,0:T(8,128)(2,1)} %convert_element_type.60), calls=%async_computation.1 | async-start | bytes 196608 | tf_op jit(solution)/shard_map/all_to_all | solution.py:123
  186.6 2.1 fusion.50
  189.5 3.8 %all-to-all-done.1 = bf16[16,8,384]{2,1,0:T(8,128)(2,1)S(1)} async-done(((bf16[16,8,384]{2,1,0:T(8,128)(2,1)}), bf16[16,8,384]{2,1,0:T(8,128)(2,1)S(1)}, u32[]{:S(2)}, u32[]{:S(2)}) %all-to-all-start.1) | async-done | bytes 98336 | tf_op jit(solution)/shard_map/all_to_all | solution.py:123
  193.3 3.5 %all-to-all-start.2 = ((bf16[16,8,384]{2,1,0:T(8,128)(2,1)}), bf16[16,8,384]{2,1,0:T(8,128)(2,1)S(1)}, u32[]{:S(2)}, u32[]{:S(2)}) async-start(bf16[16,8,384]{2,1,0:T(8,128)(2,1)} %convert_element_type.64), calls=%async_computation.2 | async-start | bytes 196608 | tf_op jit(solution)/shard_map/all_to_all | solution.py:124
  196.8 6.6 %all-to-all-done.2 = bf16[16,8,384]{2,1,0:T(8,128)(2,1)S(1)} async-done(((bf16[16,8,384]{2,1,0:T(8,128)(2,1)}), bf16[16,8,384]{2,1,0:T(8,128)(2,1)S(1)}, u32[]{:S(2)}, u32[]{:S(2)}) %all-to-all-start.2) | async-done | bytes 98336 | tf_op jit(solution)/shard_map/all_to_all | solution.py:124
  (121 shorter events, 27.5 us)
Async XLA Ops:
  7.2 8.2 %copy-start = (s32[48,16,16]{0,2,1:T(8,128)S(1)}, s32[48,16,16]{0,2,1:T(8,128)}, u32[]{:S(2)}) copy-start(s32[48,16,16]{0,2,1:T(8,128)} %param.16) | copy-start | bytes 147460
  7.2 46.5 %all-gather.5.cloned.1.call-start = ((), (), s32[]{:S(2)}) async-start(), calls=%async_computation.3 | async-start | bytes 1671168 | tf_op jit(solution)/shard_map/all_gather | solution.py:33
  8.9 85.5 %all-gather.7.cloned.1.call-start = ((), (), s32[]{:S(2)}) async-start(), calls=%async_computation.4 | async-start | bytes 1671168 | tf_op jit(solution)/shard_map/all_gather | solution.py:34
  10.6 138.6 %all-gather.9.cloned.1.call-start = ((), (), s32[]{:S(2)}) async-start(), calls=%async_computation.5 | async-start | bytes 1671168 | tf_op jit(solution)/shard_map/all_gather | solution.py:98
  12.3 162.8 %all-gather.11.cloned.1.call-start = ((), (), s32[]{:S(2)}) async-start(), calls=%async_computation.6 | async-start | bytes 1671168 | tf_op jit(solution)/shard_map/all_gather | solution.py:99
  94.4 7.0 %copy-start.1 = (bf16[128,384]{0,1:T(8,128)(2,1)S(1)}, bf16[128,384]{0,1:T(8,128)(2,1)}, u32[]{:S(2)}) copy-start(bf16[128,384]{0,1:T(8,128)(2,1)} %copy.93) | copy-start | bytes 294916
  101.5 47.7 %copy-start.3 = (bf16[128,384]{0,1:T(8,128)(2,1)S(1)}, bf16[128,384]{0,1:T(8,128)(2,1)}, u32[]{:S(2)}) copy-start(bf16[128,384]{0,1:T(8,128)(2,1)} %copy.85) | copy-start | bytes 294916
  110.8 69.1 %all-to-all-start = ((bf16[16,8,384]{2,1,0:T(8,128)(2,1)}), bf16[16,8,384]{2,1,0:T(8,128)(2,1)}, u32[]{:S(2)}, u32[]{:S(2)}) async-start(bf16[16,8,384]{2,1,0:T(8,128)(2,1)} %convert_element_type.56), calls=%async_computation | async-start | bytes 196608 | tf_op jit(solution)/shard_map/all_to_all | solution.py:122
  149.2 25.9 %copy-start.2 = (bf16[128,384]{0,1:T(8,128)(2,1)S(1)}, bf16[128,384]{0,1:T(8,128)(2,1)}, u32[]{:S(2)}) copy-start(bf16[128,384]{0,1:T(8,128)(2,1)} %copy.92) | copy-start | bytes 294916
  179.9 13.3 %all-to-all-start.1 = ((bf16[16,8,384]{2,1,0:T(8,128)(2,1)}), bf16[16,8,384]{2,1,0:T(8,128)(2,1)S(1)}, u32[]{:S(2)}, u32[]{:S(2)}) async-start(bf16[16,8,384]{2,1,0:T(8,128)(2,1)} %convert_element_type.60), calls=%async_computation.1 | async-start | bytes 196608 | tf_op jit(solution)/shard_map/all_to_all | solution.py:123
  193.3 10.1 %all-to-all-start.2 = ((bf16[16,8,384]{2,1,0:T(8,128)(2,1)}), bf16[16,8,384]{2,1,0:T(8,128)(2,1)S(1)}, u32[]{:S(2)}, u32[]{:S(2)}) async-start(bf16[16,8,384]{2,1,0:T(8,128)(2,1)} %convert_element_type.64), calls=%async_computation.2 | async-start | bytes 196608 | tf_op jit(solution)/shard_map/all_to_all | solution.py:124
Sparse Core Ops, SparseCore 0:
  10.3 43.3 all-gather.4
  56.0 38.3 all-gather.6
  96.8 38.3 all-gather.8
  136.8 38.2 all-gather.10
where the time goes:
time: 214 us; the launch traced here: 213 us
  waiting for transfers between devices  93.3 us (44%)
  blocking collectives  31.6 us (15%)
  matrix products  27.4 us (13%)
  local copies, waits for them, and re-layouts  24.5 us (11%)
  starting transfers between devices  17 us (8%)
  between operations  14 us (7%)
  other arithmetic  4.07 us (2%)
    all_gather x1, waiting for transfers between devices, local(): lax.all_gather(v_local, 'blk', axis=0, tiled=True)  34.5 us
    all_gather x1, waiting for transfers between devices, local(): lax.all_gather(k_local, 'blk', axis=0, tiled=True)  28.1 us
    all_gather x1, waiting for transfers between devices, local(): g_piece = lax.all_gather(g_local, 'blk', axis=0, tiled=True)  20.3 us
    all_gather x1, blocking collectives, local(): lax.all_gather(delta.T, 'blk', axis=0, tiled=True)  17.1 us
    all_gather x1, blocking collectives, local(): lax.all_gather(lse.T, 'blk', axis=0, tiled=True)  14.5 us
    unnamed x20, local copies, waits for them, and re-layouts  13.6 us
    dot_general x9, matrix products, scaled_scores(): jnp.einsum('qhd,khd->hqk', left, right, preferred_element_type=jnp.float32)  9.03 us
    all_to_all x1, starting transfers between devices, local(): lax.all_to_all(grad_q_b, 'uly', split_axis=0, concat_axis=1, tiled=True)  6.72 us
  transfers between devices with their start and end apart: 7, of which 5 were waited for; matrix products, arithmetic and copies ran while one was open for 24% of the time, Pallas kernels for 0%

commit v1 on v0

v1 whole, which is shorter than its diff:
```python
import functools

import jax
import jax.numpy as jnp
from jax import lax
from jax.experimental import pallas as pl
from jax.experimental.pallas import tpu as pltpu
from jax.sharding import PartitionSpec as P

H = 48
DH = 128
TILE = 128
NZ = 8
NU = 16
SLOTS = 2
WIDE = 6
COUNT = 32
MESH = pl.DeviceIdType.MESH
FACTOR = DH ** -0.5
LOG2E = 1.4426950408889634
F32 = jnp.float32
BF16 = jnp.bfloat16


def nt(a, b):
    return lax.dot_general(a, b, (((1,), (1,)), ((), ())), preferred_element_type=F32)


def nn(a, b):
    return lax.dot_general(a, b, (((1,), (0,)), ((), ())), preferred_element_type=F32)


def lift(u):
    x, y = lax.rem(u, 4), lax.div(u, 4)
    return lax.rem(2 * x + 4 * lax.rem(y, 2) + lax.div(y, 2), NZ)


def beside(u):
    x, y = lax.rem(u, 4), lax.div(u, 4)
    other = y + 1 - 2 * lax.rem(y, 2)
    return 4 * y + lax.rem(x + 1, 4), 4 * other + x, 4 * y + lax.rem(x + 3, 4)


def hosted(z, u):
    rel = lax.rem(z - lift(u) + NZ, NZ)
    yes = jnp.logical_or(rel == 0, jnp.logical_or(rel == 3, rel == 6))
    return yes, lax.div(rel, 3)


def remote(src, dst, send, recv, there):
    return pltpu.make_async_remote_copy(
        src_ref=src, dst_ref=dst, send_sem=send, recv_sem=recv,
        device_id=there, device_id_type=MESH,
    )


def arrived(ref, sem):
    pltpu.make_async_copy(ref, ref, sem).wait()


def place():
    blk = lax.axis_index("blk")
    u = lax.axis_index("uly")
    z = lax.div(blk, 2)
    c = lax.rem(blk, 2)
    yes, mine = hosted(z, u)
    return blk, u, z, c, jnp.logical_and(yes, c == lax.rem(mine, 2)), mine


def collect(
    q_in, k_in, v_in, g_in, mask_in, order_ref, kv, qg, picked,
    mask, passing, in_send, kv_sem, qg_sem, mask_sem, pass_sem, pass_send,
):
    blk, u, z, c, is_host, mine = place()
    via = beside(u)
    served = (via[2], via[1], via[0])
    barrier = pltpu.get_barrier_semaphore()

    def greet(there):
        pl.semaphore_signal(barrier, inc=1, device_id=there, device_id_type=MESH)

    get_mask = pltpu.make_async_copy(mask_in, mask, mask_sem)

    @pl.when(is_host)
    def _():
        get_mask.start()

        def greet_line(n, carry):
            greet((lax.rem(blk + n, 2 * NZ), u))
            return carry

        lax.fori_loop(1, 2 * NZ, greet_line, 0)

    for line in served:
        greet((blk, line))

    pl.semaphore_wait(barrier, 3 + 3 - is_host.astype(jnp.int32))

    def inputs(l):
        host = lax.rem(lift(u) + 3 * l, NZ)
        r = lax.rem(z - host + NZ, NZ)
        cols = pl.ds(l * DH, DH)
        there = (2 * host + l % 2, u)
        home = (
            (k_in, kv.at[c, r, 0], kv_sem),
            (v_in, kv.at[c, r, 1], kv_sem),
            (q_in, qg.at[c, r, 0], qg_sem),
            (g_in, qg.at[c, r, 1], qg_sem),
        )
        home = [(src.at[:, cols], dst, sem) for src, dst, sem in home]
        straight = [(src, dst, in_send, sem, there) for src, dst, sem in home]
        around = [
            (home[n + 1][0], passing.at[n, l], in_send, pass_sem.at[n, l], (blk, via[n]))
            for n in range(3)
        ] + straight[:1]
        return host, home, straight, around

    for l in range(3):
        host, home, straight, around = inputs(l)

        @pl.when(host != z)
        def _():
            for move in around:
                remote(*move).start()

        @pl.when(jnp.logical_and(host == z, c != l % 2))
        def _():
            for move in straight:
                remote(*move).start()

        @pl.when(jnp.logical_and(host == z, c == l % 2))
        def _():
            for move in home:
                pltpu.make_async_copy(*move).start()

    @pl.when(is_host)
    def _():
        row = lax.broadcasted_iota(jnp.int32, (16, 16), 0)
        lane = lax.broadcasted_iota(jnp.int32, (16, 16), 1)
        ident = jnp.zeros((16, 16), jnp.int32)
        for j in range(16):
            ident = jnp.where(row == j, order_ref[2 * lax.rem(z + j % NZ, NZ) + j // NZ], ident)
        hot = jnp.where(lane == ident, 1.0, 0.0).astype(BF16)
        wide = lax.broadcasted_iota(jnp.int32, (16, 128), 1)
        hot_wide = jnp.where(wide == ident[:, :1], 1.0, 0.0).astype(BF16)
        get_mask.wait()
        flat = jnp.where(mask[...] > 0, 1.0, 0.0).reshape(256, H).astype(BF16)
        head = lax.broadcasted_iota(jnp.int32, (H, 128), 0) == 3 * u + mine
        picked_out = nn(flat, jnp.where(head, 1.0, 0.0).astype(BF16))
        tall = lax.broadcasted_iota(jnp.int32, (16, 16, 128), 1)
        across = lax.broadcasted_iota(jnp.int32, (16, 16, 128), 2)
        table = jnp.where(tall == across, picked_out.reshape(16, 16, 128), 0.0)
        table = jnp.sum(table, axis=1).astype(BF16)
        by_query = nn(hot, table).astype(BF16)
        allowed = nt(by_query, hot_wide)
        before = jnp.where(row < lane, 1.0, 0.0).astype(BF16)
        rank = nn(allowed.astype(BF16), before)
        listed = jnp.where(wide == COUNT, jnp.sum(allowed, axis=1, keepdims=True), 0.0)
        for n in range(16):
            here = jnp.logical_and(allowed > 0.5, jnp.abs(rank - n) < 0.5)
            one = jnp.sum(jnp.where(here, lane.astype(F32), 0.0), axis=1, keepdims=True)
            listed = jnp.where(wide == n, one, listed)
        picked[...] = listed.astype(jnp.int32)

    def passed(n, l):
        host = lax.rem(lift(served[n]) + 3 * l, NZ)
        r = lax.rem(z - host + NZ, NZ)
        dst, sem = (
            (kv.at[c, r, 1], kv_sem),
            (qg.at[c, r, 0], qg_sem),
            (qg.at[c, r, 1], qg_sem),
        )[n]
        there = (2 * host + l % 2, served[n])
        return host != z, remote(passing.at[n, l], dst, pass_send.at[n, l], sem, there)

    for l in range(3):
        for n in range(3):
            on, move = passed(n, l)

            @pl.when(on)
            def _():
                arrived(passing.at[n, l], pass_sem.at[n, l])
                move.start()

    @pl.when(is_host)
    def _():
        arrived(kv, kv_sem)
        arrived(qg, qg_sem)
        arrived(kv.at[0, pl.ds(0, 4)], in_send)

    @pl.when(jnp.logical_not(is_host))
    def _():
        arrived(kv.at[0, pl.ds(0, 6)], in_send)

    for l in range(3):
        for n in range(3):
            on, move = passed(n, l)
            pl.when(on)(move.wait_send)


def gradients(
    kv, qg, picked_in, dq_out, kv_out,
    picked, item_row, item_base, e_buf, d_buf, top_buf, row_top, row_sum, row_mix, dq_acc, acc, sem,
):
    blk, u, z, c, is_host, mine = place()

    @pl.when(is_host)
    def _():
        get = pltpu.make_async_copy(picked_in, picked, sem)
        get.start()
        acc[...] = jnp.zeros_like(acc)
        dq_acc[...] = jnp.zeros_like(dq_acc)
        row_top[...] = jnp.full_like(row_top, -1e30)
        row_sum[...] = jnp.zeros_like(row_sum)
        row_mix[...] = jnp.zeros_like(row_mix)
        get.wait()

        items = jnp.int32(0)
        for r in range(16):
            groups = lax.div(picked[r, COUNT] + SLOTS - 1, SLOTS)

            def add(b, n, r=r):
                item_row[n] = r
                item_base[n] = b * SLOTS
                return n + 1

            items = lax.fori_loop(0, groups, add, items)
        for m in range(WIDE - 1):
            item_row[items + m] = 0
            item_base[items + m] = 16
        rounds = lax.div(items + WIDE - 1, WIDE)

        def tiles(ref, r, base, part):
            return jnp.concatenate(
                [ref[picked[r, base + m], part] for m in range(SLOTS)], axis=0
            )

        def weigh(t, carry):
            for w in range(WIDE):
                i = t * WIDE + w
                r = item_row[i]
                base = item_base[i]
                scores = nt(tiles(kv, r, base, 0), qg[r, 0]) * (FACTOR * LOG2E)
                scores = jnp.concatenate(
                    [
                        scores[128 * m:128 * m + 128]
                        + jnp.where(base + m < picked[r, COUNT], 0.0, -1e30)
                        for m in range(SLOTS)
                    ],
                    axis=0,
                )
                top = jnp.max(scores, axis=0, keepdims=True)
                e = jnp.exp2(scores - top)
                dprob = nt(tiles(kv, r, base, 1), qg[r, 1])
                e_buf[i] = e
                d_buf[i] = dprob
                top_buf[i] = top
                total = jnp.sum(e, axis=0, keepdims=True)
                mixed = jnp.sum(e * dprob, axis=0, keepdims=True)
                old = row_top[r]
                new = jnp.maximum(old, top)
                keep = jnp.exp2(old - new)
                part = jnp.exp2(top - new)
                row_top[r] = new
                row_sum[r] = row_sum[r] * keep + total * part
                row_mix[r] = row_mix[r] * keep + mixed * part
            return carry

        lax.fori_loop(0, rounds, weigh, 0)

        def spread(t, carry):
            for w in range(WIDE):
                i = t * WIDE + w
                r = item_row[i]
                base = item_base[i]
                whole = 1.0 / row_sum[r]
                prob = e_buf[i] * (jnp.exp2(top_buf[i] - row_top[r]) * whole)
                dscore = (prob * (d_buf[i] - row_mix[r] * whole)).astype(BF16)
                dk = nn(dscore, qg[r, 0])
                dv = nn(prob.astype(BF16), qg[r, 1])
                dq_acc[r] += lax.dot_general(
                    dscore, tiles(kv, r, base, 0), (((0,), (0,)), ((), ())),
                    preferred_element_type=F32,
                )
                for m in range(SLOTS):
                    j = picked[r, base + m]
                    acc[j, 0] += dk[128 * m:128 * m + 128]
                    acc[j, 1] += dv[128 * m:128 * m + 128]
            return carry

        lax.fori_loop(0, rounds, spread, 0)
        dq_out[...] = (dq_acc[...] * FACTOR).astype(BF16)

        def stage(j, carry):
            dk = acc[j, 0] * FACTOR
            dv = acc[j, 1]
            for n in range(NU):
                piece = jnp.concatenate([dk[8 * n:8 * n + 8], dv[8 * n:8 * n + 8]], axis=0)
                kv_out[NU * lax.div(j, NZ) + n, lax.rem(j, NZ)] = piece.astype(BF16)
            return carry

        lax.fori_loop(0, 16, stage, 0)


def give_back(
    dq_in, kv_out, out_q, out_k, out_v, r_q, r_kv, t_q, f_q, f_kv,
    p1q_send, p1k_send, rq_sem, rkv_sem, p2q_send, p2k_send, fq_sem, fkv_sem,
):
    blk, u, z, c, is_host, mine = place()
    seat = mine * 2 + lax.rem(lax.div(u, 4), 2)
    barrier = pltpu.get_barrier_semaphore()

    def greet(there):
        pl.semaphore_signal(barrier, inc=1, device_id=there, device_id_type=MESH)

    def greet_line(r, carry):
        greet((2 * lax.rem(z + r, NZ) + c, u))
        return carry

    def greet_plane(n, carry):
        greet((blk, lax.rem(u + n, NU)))
        return carry

    for l in range(3):
        at_line = (2 * lax.rem(lift(u) + 3 * l, NZ) + l % 2, u)
        pl.when(at_line[0] != blk)(functools.partial(greet, at_line))
        up = lax.rem(z - 3 * l + 2 * NZ, NZ)
        for half in range(2):
            x = lax.div(lax.rem(up - lax.rem(up, 2) - 4 * half + NZ, NZ), 2)
            line = 4 * (2 * lax.rem(up, 2) + half) + x
            away = jnp.logical_or(line != u, c != l % 2)
            pl.when(away)(functools.partial(greet, (2 * z + l % 2, line)))
    lax.fori_loop(1, NZ, greet_line, 0)
    lax.fori_loop(1, NU, greet_plane, 0)
    pl.semaphore_wait(barrier, 7 + 15 + (15 + 31) * is_host.astype(jnp.int32))

    @pl.when(is_host)
    def _():
        def send_k(n):
            part = pl.ds(4 * n, 4)
            for side in range(2):

                def one(i, carry):
                    to = lax.rem(u + i, NU)
                    remote(
                        kv_out.at[NU * side + to, part], r_kv.at[seat, part],
                        p1k_send.at[n], rkv_sem.at[n], (2 * z + side, to),
                    ).start()
                    return carry

                lax.fori_loop(1, NU, one, 0)

                @pl.when(c != side)
                def _():
                    one(0, 0)

                @pl.when(c == side)
                def _():
                    pltpu.make_async_copy(
                        kv_out.at[NU * side + u, part], r_kv.at[seat, part], rkv_sem.at[n]
                    ).start()

        def send_q(n, carry):
            there = lax.rem(blk + n, 2 * NZ)
            r = lax.rem(lax.div(there, 2) - z + NZ, NZ)
            tile = NZ * lax.rem(there, 2) + r
            remote(dq_in.at[tile], r_q.at[mine], p1q_send, rq_sem, (there, u)).start()
            return carry

        send_k(0)
        lax.fori_loop(1, 2 * NZ, send_q, 0)
        pltpu.make_async_copy(dq_in.at[NZ * c], r_q.at[mine], rq_sem).start()
        send_k(1)

    arrived(r_q, rq_sem)
    heads = [r_q[l].astype(F32) for l in range(3)]
    for i in range(NU):
        rows = slice(8 * i, 8 * i + 8)
        t_q[i, :16] = jnp.concatenate([heads[0][rows], heads[1][rows]], axis=0).astype(BF16)
        t_q[i, 16:] = jnp.concatenate([heads[2][rows], heads[2][rows]], axis=0).astype(BF16)

    def pass_q(i, carry):
        to = lax.rem(u + i, NU)
        remote(t_q.at[to], f_q.at[u], p2q_send, fq_sem, (blk, to)).start()
        return carry

    lax.fori_loop(1, NU, pass_q, 0)
    pltpu.make_async_copy(t_q.at[u], f_q.at[u], fq_sem).start()

    def pass_k(r, carry):
        there = (2 * lax.rem(z + r, NZ) + c, u)
        remote(r_kv.at[:, r], f_kv.at[z], p2k_send, fkv_sem, there).start()
        return carry

    arrived(r_kv.at[:, pl.ds(0, 4)], rkv_sem.at[0])
    lax.fori_loop(1, 4, pass_k, 0)
    pltpu.make_async_copy(r_kv.at[:, 0], f_kv.at[z], fkv_sem).start()
    arrived(r_kv.at[:, pl.ds(4, 4)], rkv_sem.at[1])
    lax.fori_loop(4, NZ, pass_k, 0)

    @pl.when(is_host)
    def _():
        arrived(dq_in.at[pl.ds(0, 15)], p1q_send)
        for n in range(2):
            arrived(kv_out.at[pl.ds(0, 31), pl.ds(4 * n, 4)], p1k_send.at[n])

    arrived(t_q.at[pl.ds(0, NU - 1)], p2q_send)
    arrived(r_kv.at[:, pl.ds(0, NZ - 1)], p2k_send)
    def columns(head):
        return slice(head * DH, head * DH + DH)

    arrived(f_q, fq_sem)
    for n in range(NU):
        first = f_q[n, :16].astype(F32)
        out_q[:, columns(3 * n)] = first[:8].astype(BF16)
        out_q[:, columns(3 * n + 1)] = first[8:].astype(BF16)
        out_q[:, columns(3 * n + 2)] = f_q[n, 16:].astype(F32)[:8].astype(BF16)
    arrived(f_kv, fkv_sem)
    for d in range(NZ):
        for l in range(3):
            for half in range(2):
                both = f_kv[d, 2 * l + half].astype(F32)
                up = (d - 3 * l) % NZ
                x = (up - up % 2 - 4 * half) % NZ // 2
                head = 3 * (4 * (2 * (up % 2) + half) + x) + l
                out_k[:, columns(head)] = both[:8].astype(BF16)
                out_v[:, columns(head)] = both[8:].astype(BF16)


def local(query, key, value, grad_out, tile_mask, tile_order):
    anywhere = pl.BlockSpec(memory_space=pl.ANY)
    vmem = pl.BlockSpec(memory_space=pltpu.VMEM)
    smem = pl.BlockSpec(memory_space=pltpu.SMEM)
    dma = pltpu.SemaphoreType.DMA
    shape = jax.ShapeDtypeStruct
    most = 16 * 16 // SLOTS + WIDE
    operands = (query, key, value, grad_out, jnp.transpose(tile_mask, (1, 2, 0)), tile_order)
    kv, qg, picked = pl.pallas_call(
        collect,
        out_shape=(
            shape((2, NZ, 2, 128, 128), BF16),
            shape((2, NZ, 2, 128, 128), BF16),
            shape((16, 128), jnp.int32),
        ),
        in_specs=[anywhere] * 5 + [smem],
        out_specs=(vmem, vmem, vmem),
        scratch_shapes=[
            pltpu.VMEM((16, 16, H), jnp.int32),
            pltpu.VMEM((3, 3, 128, 128), BF16),
            dma, dma, dma, dma, dma((3, 3)), dma((3, 3)),
        ],
        compiler_params=pltpu.CompilerParams(
            collective_id=0, has_side_effects=True, vmem_limit_bytes=16 * 1024 * 1024
        ),
    )(*[pltpu.with_memory_space_constraint(a, pltpu.HBM) for a in operands])
    dq, kv_out = pl.pallas_call(
        gradients,
        out_shape=(
            shape((16, 128, 128), BF16),
            shape((2 * NU, NZ, 16, 128), BF16),
        ),
        in_specs=[vmem, vmem, anywhere],
        out_specs=(vmem, vmem),
        scratch_shapes=[
            pltpu.SMEM((16, 128), jnp.int32),
            pltpu.SMEM((most,), jnp.int32),
            pltpu.SMEM((most,), jnp.int32),
            pltpu.VMEM((most, 128 * SLOTS, 128), F32),
            pltpu.VMEM((most, 128 * SLOTS, 128), F32),
            pltpu.VMEM((most, 1, 128), F32),
            pltpu.VMEM((16, 1, 128), F32),
            pltpu.VMEM((16, 1, 128), F32),
            pltpu.VMEM((16, 1, 128), F32),
            pltpu.VMEM((16, 128, 128), F32),
            pltpu.VMEM((16, 2, 128, 128), F32),
            dma,
        ],
        compiler_params=pltpu.CompilerParams(vmem_limit_bytes=48 * 1024 * 1024),
    )(kv.reshape(16, 2, 128, 128), qg.reshape(16, 2, 128, 128), picked)
    out = shape((8, H * DH), BF16)
    return pl.pallas_call(
        give_back,
        out_shape=(out, out, out),
        in_specs=[vmem] * 2,
        out_specs=(vmem, vmem, vmem),
        scratch_shapes=[
            pltpu.VMEM((3, 128, 128), BF16),
            pltpu.VMEM((6, NZ, 16, 128), BF16),
            pltpu.VMEM((NU, 32, 128), BF16),
            pltpu.VMEM((NU, 32, 128), BF16),
            pltpu.VMEM((NZ, 6, 16, 128), BF16),
            dma, dma((2,)), dma, dma((2,)), dma, dma, dma, dma,
        ],
        compiler_params=pltpu.CompilerParams(
            collective_id=1, has_side_effects=True, vmem_limit_bytes=16 * 1024 * 1024
        ),
    )(dq, kv_out)


def solution(mesh):
    placed = (P("blk", "uly"), P("blk", "uly"), P("blk", "uly"), P("blk", "uly"), P(), P())
    return jax.shard_map(
        local,
        mesh=mesh,
        in_specs=placed,
        out_specs=(P(("blk", "uly"), None), P(("blk", "uly"), None), P(("blk", "uly"), None)),
        check_vma=False,
    )
```

time: 214 us -> 51.3 us (0.24)
  waiting for transfers between devices: 93.3 us -> 0 us
  Pallas kernels: 0 us -> 48.6 us
  blocking collectives: 31.6 us -> 0 us
  matrix products: 27.4 us -> 0 us
  local copies, waits for them, and re-layouts: 24.5 us -> 1.92 us
  starting transfers between devices: 17 us -> 0 us
  between operations: 14 us -> 0.66 us
  other arithmetic: 4.07 us -> 0 us
    all_gather x4 -> x0, waiting for transfers between devices: 82.9 us -> none  [the longest x1 34.5 us: local(): lax.all_gather(v_local, 'blk', axis=0, tiled=True)]
    pallas_call x0 -> x3, Pallas kernels: none -> 48.6 us  [the longest x1 27.4 us: local(): pl.pallas_call(give_back, out_shape=(out, out, out), in_specs=[vmem] * 2,...]
    all_gather x2 -> x0, blocking collectives: 31.6 us -> none  [the longest x1 17.1 us: local(): lax.all_gather(delta.T, 'blk', axis=0, tiled=True)]
    dot_general x19 -> x0, matrix products: 27.4 us -> none  [the longest x9 9.03 us: scaled_scores(): jnp.einsum('qhd,khd->hqk', left, right, preferred_element_type=jnp.float32)]
    all_to_all x3 -> x0, starting transfers between devices: 16.9 us -> none  [the longest x1 6.72 us: local(): lax.all_to_all(grad_q_b, 'uly', split_axis=0, concat_axis=1, tiled=True)]
    unnamed x20 -> x3, local copies, waits for them, and re-layouts: 13.6 us -> 1.92 us
    all_to_all x3 -> x0, waiting for transfers between devices: 10.4 us -> none  [the longest x1 6.63 us: local(): lax.all_to_all(grad_v_b, 'uly', split_axis=0, concat_axis=1, tiled=True)]
    gather x3 -> x0, local copies, waits for them, and re-layouts: 6.64 us -> none  [the longest x1 5.46 us: local(): row_mask = jnp.take(key_mask, tile_rows, axis=1)]
  transfers between devices with their start and end apart: 7 -> 0, of which waited for: 5 -> 0; matrix products, arithmetic and copies ran while one was open for 24% -> 0% of each run, Pallas kernels for 0% -> 0%
where the time goes in v1:
time: 51.3 us; the launch traced here: 51.2 us
  Pallas kernels  48.6 us (95%)
  local copies, waits for them, and re-layouts  1.92 us (4%)
  between operations  0.66 us (1%)
    pallas_call x1, Pallas kernels, local(): pl.pallas_call(give_back, out_shape=(out, out, out), in_specs=[vmem] * 2,...  27.4 us
    pallas_call x1, Pallas kernels, local(): pl.pallas_call(collect, out_shape=(shape((2, NZ, 2, 128, 128), BF16), sha...  21.2 us
    unnamed x3, local copies, waits for them, and re-layouts  1.92 us

profile of v1, /device:TPU:1, one launch (start us, length us, event | category | flops | bytes accessed | tf_op | source)
XLA Modules:
  0.0 51.2 jit_solution(12731800928970463934)
XLA Ops:
  0.6 21.2 %shard_map.85 = (bf16[2,8,2,128,128]{4,3,2,1,0:T(8,128)(2,1)S(1)}, bf16[2,8,2,128,128]{4,3,2,1,0:T(8,128)(2,1)S(1)}, s32[16,128]{1,0:T(8,128)S(1)}) custom-call(bf16[128,384]{1,0:T(8,128)(2,1)} %q_in.1, bf16[128,384]{1,0:T(8,128)(2,1)} %k_in.1, bf16[128,384]{1,0:T(8,128)(2,1)} %v_in.1, bf16[128,384]{1,0:T(8,128)(2,1)} %g_in.1, s32[16,16,48]{2,1,0:T(8,128)} %bitcast.5, ...), custom_call_target="tpu_custom_call" | custom-call | tf_op jit(solution)/shard_map/pallas_call | solution.py:438
  21.9 27.4 %shard_map.87 = (bf16[8,6144]{1,0:T(8,128)(2,1)S(1)}, bf16[8,6144]{1,0:T(8,128)(2,1)S(1)}, bf16[8,6144]{1,0:T(8,128)(2,1)S(1)}) custom-call(bf16[16,128,128]{2,1,0:T(8,128)(2,1)S(1)} %get-tuple-element.11.dq_in, bf16[32,8,16,128]{3,2,1,0:T(8,128)(2,1)S(1)} %get-tuple-element.12.kv_out), custom_call_target="tpu_custom_call" | custom-call | tf_op jit(solution)/shard_map/pallas_call | solution.py:481
  49.3 0.6 %copy.12 = bf16[8,6144]{1,0:T(8,128)(2,1)} copy(bf16[8,6144]{1,0:T(8,128)(2,1)S(1)} %get-tuple-element.16) | data formatting | bytes 196608
  49.9 0.6 %copy.13 = bf16[8,6144]{1,0:T(8,128)(2,1)} copy(bf16[8,6144]{1,0:T(8,128)(2,1)S(1)} %get-tuple-element.17) | data formatting | bytes 196608
  50.5 0.6 %copy.14 = bf16[8,6144]{1,0:T(8,128)(2,1)} copy(bf16[8,6144]{1,0:T(8,128)(2,1)S(1)} %get-tuple-element.18) | data formatting | bytes 196608
  (1 shorter events, 0.0 us)

commit v2 on v1

--- a/solution.py
+++ b/solution.py
@@ -99,8 +99,8 @@
     def inputs(l):
         host = lax.rem(lift(u) + 3 * l, NZ)
         r = lax.rem(z - host + NZ, NZ)
-        cols = pl.ds(l * DH, DH)
-        there = (2 * host + l % 2, u)
+        cols = pl.ds(pl.multiple_of(l * DH, DH), DH)
+        there = (2 * host + lax.rem(l, 2), u)
         home = (
             (k_in, kv.at[c, r, 0], kv_sem),
             (v_in, kv.at[c, r, 1], kv_sem),
@@ -115,7 +115,11 @@
         ] + straight[:1]
         return host, home, straight, around
 
-    for l in range(3):
+    def nth(n, line):
+        return lax.rem(z + line + n, 3)
+
+    for n in range(3):
+        l = nth(n, u)
         host, home, straight, around = inputs(l)
 
         @pl.when(host != z)
@@ -123,12 +127,12 @@
             for move in around:
                 remote(*move).start()
 
-        @pl.when(jnp.logical_and(host == z, c != l % 2))
+        @pl.when(jnp.logical_and(host == z, c != lax.rem(l, 2)))
         def _():
             for move in straight:
                 remote(*move).start()
 
-        @pl.when(jnp.logical_and(host == z, c == l % 2))
+        @pl.when(jnp.logical_and(host == z, c == lax.rem(l, 2)))
         def _():
             for move in home:
                 pltpu.make_async_copy(*move).start()
@@ -170,11 +174,12 @@
             (qg.at[c, r, 0], qg_sem),
             (qg.at[c, r, 1], qg_sem),
         )[n]
-        there = (2 * host + l % 2, served[n])
+        there = (2 * host + lax.rem(l, 2), served[n])
         return host != z, remote(passing.at[n, l], dst, pass_send.at[n, l], sem, there)
 
-    for l in range(3):
+    for i in range(3):
         for n in range(3):
+            l = nth(i, served[n])
             on, move = passed(n, l)
 
             @pl.when(on)
@@ -199,8 +204,8 @@
 
 
 def gradients(
-    kv, qg, picked_in, dq_out, kv_out,
-    picked, item_row, item_base, e_buf, d_buf, top_buf, row_top, row_sum, row_mix, dq_acc, acc, sem,
+    kv, qg, picked_in, dq_out, acc,
+    picked, item_row, item_base, e_buf, d_buf, top_buf, row_top, row_sum, row_mix, dq_acc, sem,
 ):
     blk, u, z, c, is_host, mine = place()
 
@@ -291,19 +296,9 @@
         lax.fori_loop(0, rounds, spread, 0)
         dq_out[...] = (dq_acc[...] * FACTOR).astype(BF16)
 
-        def stage(j, carry):
-            dk = acc[j, 0] * FACTOR
-            dv = acc[j, 1]
-            for n in range(NU):
-                piece = jnp.concatenate([dk[8 * n:8 * n + 8], dv[8 * n:8 * n + 8]], axis=0)
-                kv_out[NU * lax.div(j, NZ) + n, lax.rem(j, NZ)] = piece.astype(BF16)
-            return carry
-
-        lax.fori_loop(0, 16, stage, 0)
-
 
 def give_back(
-    dq_in, kv_out, out_q, out_k, out_v, r_q, r_kv, t_q, f_q, f_kv,
+    dq_in, acc, f_q, f_kv, kv_out, r_q, r_kv, t_q,
     p1q_send, p1k_send, rq_sem, rkv_sem, p2q_send, p2k_send, fq_sem, fkv_sem,
 ):
     blk, u, z, c, is_host, mine = place()
@@ -332,33 +327,41 @@
             pl.when(away)(functools.partial(greet, (2 * z + l % 2, line)))
     lax.fori_loop(1, NZ, greet_line, 0)
     lax.fori_loop(1, NU, greet_plane, 0)
+
+    @pl.when(is_host)
+    def _():
+        def stage(j, carry):
+            dk = acc[j, 0] * FACTOR
+            dv = acc[j, 1]
+            for n in range(NU):
+                piece = jnp.concatenate([dk[8 * n:8 * n + 8], dv[8 * n:8 * n + 8]], axis=0)
+                kv_out[NU * lax.div(j, NZ) + n, lax.rem(j, NZ)] = piece.astype(BF16)
+            return carry
+
+        lax.fori_loop(0, 16, stage, 0)
+
     pl.semaphore_wait(barrier, 7 + 15 + (15 + 31) * is_host.astype(jnp.int32))
 
     @pl.when(is_host)
     def _():
-        def send_k(n):
-            part = pl.ds(4 * n, 4)
-            for side in range(2):
-
-                def one(i, carry):
-                    to = lax.rem(u + i, NU)
-                    remote(
-                        kv_out.at[NU * side + to, part], r_kv.at[seat, part],
-                        p1k_send.at[n], rkv_sem.at[n], (2 * z + side, to),
-                    ).start()
-                    return carry
-
-                lax.fori_loop(1, NU, one, 0)
-
-                @pl.when(c != side)
-                def _():
-                    one(0, 0)
-
-                @pl.when(c == side)
-                def _():
-                    pltpu.make_async_copy(
-                        kv_out.at[NU * side + u, part], r_kv.at[seat, part], rkv_sem.at[n]
-                    ).start()
+        for side in range(2):
+
+            def send_k(i, carry, side=side):
+                to = lax.rem(u + i, NU)
+                remote(
+                    kv_out.at[NU * side + to], r_kv.at[seat], p1k_send, rkv_sem, (2 * z + side, to)
+                ).start()
+                return carry
+
+            lax.fori_loop(1, NU, send_k, 0)
+
+            @pl.when(c != side)
+            def _():
+                send_k(0, 0)
+
+            @pl.when(c == side)
+            def _():
+                pltpu.make_async_copy(kv_out.at[NU * side + u], r_kv.at[seat], rkv_sem).start()
 
         def send_q(n, carry):
             there = lax.rem(blk + n, 2 * NZ)
@@ -367,10 +370,8 @@
             remote(dq_in.at[tile], r_q.at[mine], p1q_send, rq_sem, (there, u)).start()
             return carry
 
-        send_k(0)
         lax.fori_loop(1, 2 * NZ, send_q, 0)
         pltpu.make_async_copy(dq_in.at[NZ * c], r_q.at[mine], rq_sem).start()
-        send_k(1)
 
     arrived(r_q, rq_sem)
     heads = [r_q[l].astype(F32) for l in range(3)]
@@ -392,30 +393,35 @@
         remote(r_kv.at[:, r], f_kv.at[z], p2k_send, fkv_sem, there).start()
         return carry
 
-    arrived(r_kv.at[:, pl.ds(0, 4)], rkv_sem.at[0])
-    lax.fori_loop(1, 4, pass_k, 0)
+    arrived(r_kv, rkv_sem)
+    lax.fori_loop(1, NZ, pass_k, 0)
     pltpu.make_async_copy(r_kv.at[:, 0], f_kv.at[z], fkv_sem).start()
-    arrived(r_kv.at[:, pl.ds(4, 4)], rkv_sem.at[1])
-    lax.fori_loop(4, NZ, pass_k, 0)
 
     @pl.when(is_host)
     def _():
         arrived(dq_in.at[pl.ds(0, 15)], p1q_send)
-        for n in range(2):
-            arrived(kv_out.at[pl.ds(0, 31), pl.ds(4 * n, 4)], p1k_send.at[n])
-
+        arrived(kv_out.at[pl.ds(0, 31)], p1k_send)
+
+    arrived(r_kv.at[:, pl.ds(0, NZ - 1)], p2k_send)
     arrived(t_q.at[pl.ds(0, NU - 1)], p2q_send)
-    arrived(r_kv.at[:, pl.ds(0, NZ - 1)], p2k_send)
+    arrived(f_q, fq_sem)
+    arrived(f_kv, fkv_sem)
+
+
+def assemble(f_q, f_kv, q_hbm, k_hbm, v_hbm, out_q, out_k, out_v, sems):
     def columns(head):
         return slice(head * DH, head * DH + DH)
 
-    arrived(f_q, fq_sem)
+    copies = [
+        pltpu.make_async_copy(src, dst, sems.at[n])
+        for n, (src, dst) in enumerate(((out_q, q_hbm), (out_k, k_hbm), (out_v, v_hbm)))
+    ]
     for n in range(NU):
         first = f_q[n, :16].astype(F32)
         out_q[:, columns(3 * n)] = first[:8].astype(BF16)
         out_q[:, columns(3 * n + 1)] = first[8:].astype(BF16)
         out_q[:, columns(3 * n + 2)] = f_q[n, 16:].astype(F32)[:8].astype(BF16)
-    arrived(f_kv, fkv_sem)
+    copies[0].start()
     for d in range(NZ):
         for l in range(3):
             for half in range(2):
@@ -425,6 +431,10 @@
                 head = 3 * (4 * (2 * (up % 2) + half) + x) + l
                 out_k[:, columns(head)] = both[:8].astype(BF16)
                 out_v[:, columns(head)] = both[8:].astype(BF16)
+    copies[1].start()
+    copies[2].start()
+    for copy in copies:
+        copy.wait()
 
 
 def local(query, key, value, grad_out, tile_mask, tile_order):
@@ -453,11 +463,11 @@
             collective_id=0, has_side_effects=True, vmem_limit_bytes=16 * 1024 * 1024
         ),
     )(*[pltpu.with_memory_space_constraint(a, pltpu.HBM) for a in operands])
-    dq, kv_out = pl.pallas_call(
+    dq, acc = pl.pallas_call(
         gradients,
         out_shape=(
             shape((16, 128, 128), BF16),
-            shape((2 * NU, NZ, 16, 128), BF16),
+            shape((16, 2, 128, 128), F32),
         ),
         in_specs=[vmem, vmem, anywhere],
         out_specs=(vmem, vmem),
@@ -472,29 +482,35 @@
             pltpu.VMEM((16, 1, 128), F32),
             pltpu.VMEM((16, 1, 128), F32),
             pltpu.VMEM((16, 128, 128), F32),
-            pltpu.VMEM((16, 2, 128, 128), F32),
             dma,
         ],
         compiler_params=pltpu.CompilerParams(vmem_limit_bytes=48 * 1024 * 1024),
     )(kv.reshape(16, 2, 128, 128), qg.reshape(16, 2, 128, 128), picked)
-    out = shape((8, H * DH), BF16)
-    return pl.pallas_call(
+    f_q, f_kv = pl.pallas_call(
         give_back,
-        out_shape=(out, out, out),
+        out_shape=(shape((NU, 32, 128), BF16), shape((NZ, 6, 16, 128), BF16)),
         in_specs=[vmem] * 2,
-        out_specs=(vmem, vmem, vmem),
+        out_specs=(vmem, vmem),
         scratch_shapes=[
+            pltpu.VMEM((2 * NU, NZ, 16, 128), BF16),
             pltpu.VMEM((3, 128, 128), BF16),
             pltpu.VMEM((6, NZ, 16, 128), BF16),
             pltpu.VMEM((NU, 32, 128), BF16),
-            pltpu.VMEM((NU, 32, 128), BF16),
-            pltpu.VMEM((NZ, 6, 16, 128), BF16),
-            dma, dma((2,)), dma, dma((2,)), dma, dma, dma, dma,
+            dma, dma, dma, dma, dma, dma, dma, dma,
         ],
         compiler_params=pltpu.CompilerParams(
             collective_id=1, has_side_effects=True, vmem_limit_bytes=16 * 1024 * 1024
         ),
-    )(dq, kv_out)
+    )(dq, acc)
+    out = shape((8, H * DH), BF16)
+    return pl.pallas_call(
+        assemble,
+        out_shape=(out, out, out),
+        in_specs=[vmem] * 2,
+        out_specs=(anywhere, anywhere, anywhere),
+        scratch_shapes=[pltpu.VMEM((8, H * DH), BF16)] * 3 + [dma((3,))],
+        compiler_params=pltpu.CompilerParams(vmem_limit_bytes=8 * 1024 * 1024),
+    )(*[pltpu.with_memory_space_constraint(a, pltpu.VMEM) for a in (f_q, f_kv)])
 
 
 def solution(mesh):

time: 51.3 us -> 51.4 us (level)
  Pallas kernels: 48.6 us -> 50.7 us
  local copies, waits for them, and re-layouts: 1.92 us -> 0 us
    pallas_call x1 -> x2, Pallas kernels: 27.4 us -> 29.6 us  [the longest x1 28.9 us: local(): pl.pallas_call(give_back, out_shape=(shape((NU, 32, 128), BF16), shape((N...]
    unnamed x3 -> x0, local copies, waits for them, and re-layouts: 1.92 us -> none
where the time goes in v2:
time: 51.4 us; the launch traced here: 51.3 us
  Pallas kernels  50.7 us (99%)
  between operations  0.66 us (1%)
    pallas_call x1, Pallas kernels, local(): pl.pallas_call(give_back, out_shape=(shape((NU, 32, 128), BF16), shape((N...  28.9 us
    pallas_call x1, Pallas kernels, local(): pl.pallas_call(collect, out_shape=(shape((2, NZ, 2, 128, 128), BF16), sha...  21 us

profile of v2, /device:TPU:1, one launch (start us, length us, event | category | flops | bytes accessed | tf_op | source)
XLA Modules:
  0.0 51.3 jit_solution(6193995051989581487)
XLA Ops:
  0.6 21.0 %shard_map.85 = (bf16[2,8,2,128,128]{4,3,2,1,0:T(8,128)(2,1)S(1)}, bf16[2,8,2,128,128]{4,3,2,1,0:T(8,128)(2,1)S(1)}, s32[16,128]{1,0:T(8,128)S(1)}) custom-call(bf16[128,384]{1,0:T(8,128)(2,1)} %q_in.1, bf16[128,384]{1,0:T(8,128)(2,1)} %k_in.1, bf16[128,384]{1,0:T(8,128)(2,1)} %v_in.1, bf16[128,384]{1,0:T(8,128)(2,1)} %g_in.1, s32[16,16,48]{2,1,0:T(8,128)} %bitcast.5, ...), custom_call_target="tpu_custom_call" | custom-call | tf_op jit(solution)/shard_map/pallas_call | solution.py:448
  21.7 28.9 %shard_map.87 = (bf16[16,32,128]{2,1,0:T(8,128)(2,1)S(1)}, bf16[8,6,16,128]{3,2,1,0:T(8,128)(2,1)S(1)}) custom-call(bf16[16,128,128]{2,1,0:T(8,128)(2,1)S(1)} %get-tuple-element.13.dq_in, f32[16,2,128,128]{3,2,1,0:T(8,128)S(1)} %get-tuple-element.14.acc), custom_call_target="tpu_custom_call" | custom-call | tf_op jit(solution)/shard_map/pallas_call | solution.py:489
  50.6 0.8 %shard_map.88 = (bf16[8,6144]{1,0:T(8,128)(2,1)}, bf16[8,6144]{1,0:T(8,128)(2,1)}, bf16[8,6144]{1,0:T(8,128)(2,1)}) custom-call(bf16[16,32,128]{2,1,0:T(8,128)(2,1)S(1)} %get-tuple-element.15.f_q, bf16[8,6,16,128]{3,2,1,0:T(8,128)(2,1)S(1)} %get-tuple-element.16.f_kv), custom_call_target="tpu_custom_call" | custom-call | tf_op jit(solution)/shard_map/pallas_call | solution.py:506
  (1 shorter events, 0.0 us)

commit v3 on v2

--- a/solution.py
+++ b/solution.py
@@ -14,7 +14,9 @@
 NU = 16
 SLOTS = 2
 WIDE = 6
+SECOND = 16
 COUNT = 32
+EMPTY = 40
 MESH = pl.DeviceIdType.MESH
 FACTOR = DH ** -0.5
 LOG2E = 1.4426950408889634
@@ -63,79 +65,76 @@
     u = lax.axis_index("uly")
     z = lax.div(blk, 2)
     c = lax.rem(blk, 2)
-    yes, mine = hosted(z, u)
-    return blk, u, z, c, jnp.logical_and(yes, c == lax.rem(mine, 2)), mine
+    is_host, mine = hosted(z, u)
+    return blk, u, z, c, is_host, mine
 
 
 def collect(
     q_in, k_in, v_in, g_in, mask_in, order_ref, kv, qg, picked,
-    mask, passing, in_send, kv_sem, qg_sem, mask_sem, pass_sem, pass_send,
+    mask, passing, in_send, kv_sem, qg_sem, kv_send, kv_recv, qg_send, qg_recv,
+    mask_sem, pass_sem, pass_send,
 ):
     blk, u, z, c, is_host, mine = place()
+    sibling = (2 * z + 1 - c, u)
     via = beside(u)
     served = (via[2], via[1], via[0])
     barrier = pltpu.get_barrier_semaphore()
+    get_mask = pltpu.make_async_copy(mask_in, mask, mask_sem)
 
     def greet(there):
         pl.semaphore_signal(barrier, inc=1, device_id=there, device_id_type=MESH)
 
-    get_mask = pltpu.make_async_copy(mask_in, mask, mask_sem)
-
     @pl.when(is_host)
     def _():
         get_mask.start()
 
-        def greet_line(n, carry):
-            greet((lax.rem(blk + n, 2 * NZ), u))
+        def greet_line(r, carry):
+            greet((2 * lax.rem(z + r, NZ) + c, u))
             return carry
 
-        lax.fori_loop(1, 2 * NZ, greet_line, 0)
+        lax.fori_loop(1, NZ, greet_line, 0)
+        greet(sibling)
 
     for line in served:
         greet((blk, line))
 
-    pl.semaphore_wait(barrier, 3 + 3 - is_host.astype(jnp.int32))
+    pl.semaphore_wait(barrier, 6)
 
     def inputs(l):
         host = lax.rem(lift(u) + 3 * l, NZ)
         r = lax.rem(z - host + NZ, NZ)
         cols = pl.ds(pl.multiple_of(l * DH, DH), DH)
-        there = (2 * host + lax.rem(l, 2), u)
-        home = (
-            (k_in, kv.at[c, r, 0], kv_sem),
-            (v_in, kv.at[c, r, 1], kv_sem),
-            (q_in, qg.at[c, r, 0], qg_sem),
-            (g_in, qg.at[c, r, 1], qg_sem),
-        )
-        home = [(src.at[:, cols], dst, sem) for src, dst, sem in home]
-        straight = [(src, dst, in_send, sem, there) for src, dst, sem in home]
-        around = [
+        home = [
+            (src.at[:, cols], dst, sem)
+            for src, dst, sem in (
+                (k_in, kv.at[1, r, 0], kv_sem.at[r]),
+                (v_in, kv.at[1, r, 1], kv_sem.at[r]),
+                (q_in, qg.at[1, r, 0], qg_sem.at[r]),
+                (g_in, qg.at[1, r, 1], qg_sem.at[r]),
+            )
+        ]
+        away = [(*home[0][:2], in_send, home[0][2], (2 * host + c, u))] + [
             (home[n + 1][0], passing.at[n, l], in_send, pass_sem.at[n, l], (blk, via[n]))
             for n in range(3)
-        ] + straight[:1]
-        return host, home, straight, around
+        ]
+        return host, home, away
 
     def nth(n, line):
         return lax.rem(z + line + n, 3)
 
-    for n in range(3):
-        l = nth(n, u)
-        host, home, straight, around = inputs(l)
-
-        @pl.when(host != z)
-        def _():
-            for move in around:
-                remote(*move).start()
-
-        @pl.when(jnp.logical_and(host == z, c != lax.rem(l, 2)))
-        def _():
-            for move in straight:
-                remote(*move).start()
-
-        @pl.when(jnp.logical_and(host == z, c == lax.rem(l, 2)))
-        def _():
-            for move in home:
-                pltpu.make_async_copy(*move).start()
+    for part in (slice(0, 2), slice(2, 4)):
+        for n in range(3):
+            host, home, away = inputs(nth(n, u))
+
+            @pl.when(host != z)
+            def _():
+                for move in away[part]:
+                    remote(*move).start()
+
+            @pl.when(host == z)
+            def _():
+                for move in home[part]:
+                    pltpu.make_async_copy(*move).start()
 
     @pl.when(is_host)
     def _():
@@ -143,7 +142,8 @@
         lane = lax.broadcasted_iota(jnp.int32, (16, 16), 1)
         ident = jnp.zeros((16, 16), jnp.int32)
         for j in range(16):
-            ident = jnp.where(row == j, order_ref[2 * lax.rem(z + j % NZ, NZ) + j // NZ], ident)
+            side = c if j // NZ else 1 - c
+            ident = jnp.where(row == j, order_ref[2 * lax.rem(z + j % NZ, NZ) + side], ident)
         hot = jnp.where(lane == ident, 1.0, 0.0).astype(BF16)
         wide = lax.broadcasted_iota(jnp.int32, (16, 128), 1)
         hot_wide = jnp.where(wide == ident[:, :1], 1.0, 0.0).astype(BF16)
@@ -157,40 +157,60 @@
         table = jnp.sum(table, axis=1).astype(BF16)
         by_query = nn(hot, table).astype(BF16)
         allowed = nt(by_query, hot_wide)
-        before = jnp.where(row < lane, 1.0, 0.0).astype(BF16)
+        one_side = lax.div(row, NZ) == lax.div(lane, NZ)
+        before = jnp.where(jnp.logical_and(row < lane, one_side), 1.0, 0.0).astype(BF16)
         rank = nn(allowed.astype(BF16), before)
-        listed = jnp.where(wide == COUNT, jnp.sum(allowed, axis=1, keepdims=True), 0.0)
-        for n in range(16):
-            here = jnp.logical_and(allowed > 0.5, jnp.abs(rank - n) < 0.5)
-            one = jnp.sum(jnp.where(here, lane.astype(F32), 0.0), axis=1, keepdims=True)
-            listed = jnp.where(wide == n, one, listed)
+        near = jnp.where(lane >= NZ, allowed, 0.0)
+        far = jnp.where(lane >= NZ, 0.0, allowed)
+        listed = jnp.where(wide == COUNT, jnp.sum(near, axis=1, keepdims=True), 0.0)
+        ends = SECOND + jnp.sum(far, axis=1, keepdims=True)
+        listed = jnp.where(wide == COUNT + 1, ends, listed)
+        for first, some in ((0, near), (SECOND, far)):
+            for n in range(NZ):
+                here = jnp.logical_and(some > 0.5, jnp.abs(rank - n) < 0.5)
+                one = jnp.sum(jnp.where(here, lane.astype(F32), 0.0), axis=1, keepdims=True)
+                listed = jnp.where(wide == first + n, one, listed)
         picked[...] = listed.astype(jnp.int32)
 
     def passed(n, l):
         host = lax.rem(lift(served[n]) + 3 * l, NZ)
         r = lax.rem(z - host + NZ, NZ)
         dst, sem = (
-            (kv.at[c, r, 1], kv_sem),
-            (qg.at[c, r, 0], qg_sem),
-            (qg.at[c, r, 1], qg_sem),
+            (kv.at[1, r, 1], kv_sem.at[r]),
+            (qg.at[1, r, 0], qg_sem.at[r]),
+            (qg.at[1, r, 1], qg_sem.at[r]),
         )[n]
-        there = (2 * host + lax.rem(l, 2), served[n])
+        there = (2 * host + c, served[n])
         return host != z, remote(passing.at[n, l], dst, pass_send.at[n, l], sem, there)
 
-    for i in range(3):
-        for n in range(3):
-            l = nth(i, served[n])
-            on, move = passed(n, l)
-
-            @pl.when(on)
-            def _():
-                arrived(passing.at[n, l], pass_sem.at[n, l])
-                move.start()
-
-    @pl.when(is_host)
-    def _():
-        arrived(kv, kv_sem)
-        arrived(qg, qg_sem)
+    for part in ((0,), (1, 2)):
+        for i in range(3):
+            for n in part:
+                l = nth(i, served[n])
+                on, move = passed(n, l)
+
+                @pl.when(on)
+                def _():
+                    arrived(passing.at[n, l], pass_sem.at[n, l])
+                    move.start()
+
+    @pl.when(is_host)
+    def _():
+        for ref, sems, send, recv in (
+            (kv, kv_sem, kv_send, kv_recv), (qg, qg_sem, qg_send, qg_recv)
+        ):
+
+            def share(n, carry, ref=ref, sems=sems, send=send, recv=recv):
+                odd = lax.rem(n, 2)
+                r = lax.rem(odd * lax.div(n + 1, 2) + (1 - odd) * (NZ - lax.div(n, 2)), NZ)
+                arrived(ref.at[1, r], sems.at[r])
+                remote(ref.at[1, r], ref.at[0, r], send, recv, sibling).start()
+                return carry
+
+            lax.fori_loop(0, NZ, share, 0)
+        for ref, send, recv in ((kv, kv_send, kv_recv), (qg, qg_send, qg_recv)):
+            arrived(ref.at[0], recv)
+            arrived(ref.at[1], send)
         arrived(kv.at[0, pl.ds(0, 4)], in_send)
 
     @pl.when(jnp.logical_not(is_host))
@@ -205,7 +225,7 @@
 
 def gradients(
     kv, qg, picked_in, dq_out, acc,
-    picked, item_row, item_base, e_buf, d_buf, top_buf, row_top, row_sum, row_mix, dq_acc, sem,
+    picked, item_row, item_base, item_end, e_buf, d_buf, top_buf, row_top, row_sum, row_mix, dq_acc, sem,
 ):
     blk, u, z, c, is_host, mine = place()
 
@@ -213,27 +233,35 @@
     def _():
         get = pltpu.make_async_copy(picked_in, picked, sem)
         get.start()
-        acc[...] = jnp.zeros_like(acc)
-        dq_acc[...] = jnp.zeros_like(dq_acc)
+        acc[NZ:] = jnp.zeros((NZ, 2, 128, 128), F32)
+        dq_acc[NZ:] = jnp.zeros((NZ, 128, 128), F32)
         row_top[...] = jnp.full_like(row_top, -1e30)
         row_sum[...] = jnp.zeros_like(row_sum)
         row_mix[...] = jnp.zeros_like(row_mix)
         get.wait()
 
-        items = jnp.int32(0)
-        for r in range(16):
-            groups = lax.div(picked[r, COUNT] + SLOTS - 1, SLOTS)
-
-            def add(b, n, r=r):
-                item_row[n] = r
-                item_base[n] = b * SLOTS
-                return n + 1
-
-            items = lax.fori_loop(0, groups, add, items)
+        def listing(rows, first, end, items):
+            for r in rows:
+                stop = picked[r, end]
+
+                def add(b, n, r=r, stop=stop):
+                    item_row[n] = r
+                    item_base[n] = first + b * SLOTS
+                    item_end[n] = stop
+                    return n + 1
+
+                items = lax.fori_loop(0, lax.div(stop - first + SLOTS - 1, SLOTS), add, items)
+            return items
+
+        own, other = range(NZ, 16), range(NZ)
+        items = listing(own, 0, COUNT, jnp.int32(0))
+        items = listing(other, 0, COUNT, items)
+        needed = listing(own, SECOND, COUNT + 1, items)
+        items = listing(other, SECOND, COUNT + 1, needed)
         for m in range(WIDE - 1):
             item_row[items + m] = 0
-            item_base[items + m] = 16
-        rounds = lax.div(items + WIDE - 1, WIDE)
+            item_base[items + m] = EMPTY
+            item_end[items + m] = 0
 
         def tiles(ref, r, base, part):
             return jnp.concatenate(
@@ -249,7 +277,7 @@
                 scores = jnp.concatenate(
                     [
                         scores[128 * m:128 * m + 128]
-                        + jnp.where(base + m < picked[r, COUNT], 0.0, -1e30)
+                        + jnp.where(base + m < item_end[i], 0.0, -1e30)
                         for m in range(SLOTS)
                     ],
                     axis=0,
@@ -271,7 +299,7 @@
                 row_mix[r] = row_mix[r] * keep + mixed * part
             return carry
 
-        lax.fori_loop(0, rounds, weigh, 0)
+        lax.fori_loop(0, lax.div(items + WIDE - 1, WIDE), weigh, 0)
 
         def spread(t, carry):
             for w in range(WIDE):
@@ -293,85 +321,111 @@
                     acc[j, 1] += dv[128 * m:128 * m + 128]
             return carry
 
-        lax.fori_loop(0, rounds, spread, 0)
-        dq_out[...] = (dq_acc[...] * FACTOR).astype(BF16)
+        lax.fori_loop(0, lax.div(needed + WIDE - 1, WIDE), spread, 0)
+        dq_out[...] = (dq_acc[NZ:] * FACTOR).astype(BF16)
 
 
 def give_back(
     dq_in, acc, f_q, f_kv, kv_out, r_q, r_kv, t_q,
-    p1q_send, p1k_send, rq_sem, rkv_sem, p2q_send, p2k_send, fq_sem, fkv_sem,
+    p1q_send, p1k_send, rq_sem, rkv_sem, p2q_send, p2k_send, fq_sem, fkv_sem, others,
 ):
     blk, u, z, c, is_host, mine = place()
     seat = mine * 2 + lax.rem(lax.div(u, 4), 2)
+    rest = jnp.logical_not(is_host)
     barrier = pltpu.get_barrier_semaphore()
 
-    def greet(there):
-        pl.semaphore_signal(barrier, inc=1, device_id=there, device_id_type=MESH)
+    def greet(there, other):
+        @pl.when(jnp.logical_or(rest, jnp.logical_not(other)))
+        def _():
+            pl.semaphore_signal(barrier, inc=1, device_id=there, device_id_type=MESH)
 
     def greet_line(r, carry):
-        greet((2 * lax.rem(z + r, NZ) + c, u))
+        h = lax.rem(z + r, NZ)
+        greet((2 * h + c, u), hosted(h, u)[0])
         return carry
 
     def greet_plane(n, carry):
-        greet((blk, lax.rem(u + n, NU)))
+        to = lax.rem(u + n, NU)
+        greet((blk, to), hosted(z, to)[0])
         return carry
 
-    for l in range(3):
-        at_line = (2 * lax.rem(lift(u) + 3 * l, NZ) + l % 2, u)
-        pl.when(at_line[0] != blk)(functools.partial(greet, at_line))
-        up = lax.rem(z - 3 * l + 2 * NZ, NZ)
-        for half in range(2):
-            x = lax.div(lax.rem(up - lax.rem(up, 2) - 4 * half + NZ, NZ), 2)
-            line = 4 * (2 * lax.rem(up, 2) + half) + x
-            away = jnp.logical_or(line != u, c != l % 2)
-            pl.when(away)(functools.partial(greet, (2 * z + l % 2, line)))
     lax.fori_loop(1, NZ, greet_line, 0)
     lax.fori_loop(1, NU, greet_plane, 0)
 
     @pl.when(is_host)
     def _():
-        def stage(j, carry):
-            dk = acc[j, 0] * FACTOR
-            dv = acc[j, 1]
+        def stage(r, carry):
+            dk = acc[NZ + r, 0] * FACTOR
+            dv = acc[NZ + r, 1]
             for n in range(NU):
                 piece = jnp.concatenate([dk[8 * n:8 * n + 8], dv[8 * n:8 * n + 8]], axis=0)
-                kv_out[NU * lax.div(j, NZ) + n, lax.rem(j, NZ)] = piece.astype(BF16)
+                kv_out[n, lax.rem(z + r, NZ)] = piece.astype(BF16)
             return carry
 
-        lax.fori_loop(0, 16, stage, 0)
-
-    pl.semaphore_wait(barrier, 7 + 15 + (15 + 31) * is_host.astype(jnp.int32))
-
-    @pl.when(is_host)
-    def _():
-        for side in range(2):
-
-            def send_k(i, carry, side=side):
-                to = lax.rem(u + i, NU)
-                remote(
-                    kv_out.at[NU * side + to], r_kv.at[seat], p1k_send, rkv_sem, (2 * z + side, to)
-                ).start()
+        lax.fori_loop(0, NZ, stage, 0)
+
+    pl.semaphore_wait(barrier, 22 - 7 * is_host.astype(jnp.int32))
+
+    def tell(there):
+        pl.semaphore_signal(others, inc=1, device_id=there, device_id_type=MESH)
+
+    @pl.when(rest)
+    def _():
+        below = lax.rem(z + NZ - 1, NZ)
+        right, _, left = beside(u)
+        left_hosts, left_head = hosted(z, left)
+        right_hosts, right_head = hosted(z, right)
+        pl.when(hosted(below, u)[0])(functools.partial(tell, (2 * below + c, u)))
+        on = jnp.logical_and(left_hosts, left_head > 0)
+        pl.when(on)(functools.partial(tell, (blk, left)))
+        on = jnp.logical_and(right_hosts, right_head == 0)
+        pl.when(on)(functools.partial(tell, (blk, right)))
+
+    @pl.when(is_host)
+    def _():
+        def send_k(part, to_hosts):
+            heights = pl.ds(4 * part, 4)
+
+            def one(n, carry):
+                to = lax.rem(u + n, NU)
+
+                @pl.when(hosted(z, to)[0] == to_hosts)
+                def _():
+                    remote(
+                        kv_out.at[to, heights], r_kv.at[seat, heights],
+                        p1k_send, rkv_sem.at[part], (blk, to),
+                    ).start()
+
                 return carry
 
-            lax.fori_loop(1, NU, send_k, 0)
-
-            @pl.when(c != side)
-            def _():
-                send_k(0, 0)
-
-            @pl.when(c == side)
-            def _():
-                pltpu.make_async_copy(kv_out.at[NU * side + u], r_kv.at[seat], rkv_sem).start()
-
-        def send_q(n, carry):
-            there = lax.rem(blk + n, 2 * NZ)
-            r = lax.rem(lax.div(there, 2) - z + NZ, NZ)
-            tile = NZ * lax.rem(there, 2) + r
-            remote(dq_in.at[tile], r_q.at[mine], p1q_send, rq_sem, (there, u)).start()
-            return carry
-
-        lax.fori_loop(1, 2 * NZ, send_q, 0)
-        pltpu.make_async_copy(dq_in.at[NZ * c], r_q.at[mine], rq_sem).start()
+            lax.fori_loop(1, NU, one, 0)
+
+        def send_q(to_hosts):
+            def one(h, carry):
+                on = jnp.logical_and(h != z, hosted(h, u)[0] == to_hosts)
+
+                @pl.when(on)
+                def _():
+                    tile = dq_in.at[lax.rem(h - z + NZ, NZ)]
+                    remote(tile, r_q.at[mine], p1q_send, rq_sem, (2 * h + c, u)).start()
+
+                return carry
+
+            lax.fori_loop(0, NZ, one, 0)
+
+        send_k(0, False)
+        send_q(False)
+        send_k(1, False)
+        pltpu.make_async_copy(dq_in.at[0], r_q.at[mine], rq_sem).start()
+        for part in range(2):
+            heights = pl.ds(4 * part, 4)
+            pltpu.make_async_copy(
+                kv_out.at[u, heights], r_kv.at[seat, heights], rkv_sem.at[part]
+            ).start()
+        pl.semaphore_wait(others, 2)
+        send_k(0, True)
+        send_q(True)
+        send_k(1, True)
 
     arrived(r_q, rq_sem)
     heads = [r_q[l].astype(F32) for l in range(3)]
@@ -388,19 +442,25 @@
     lax.fori_loop(1, NU, pass_q, 0)
     pltpu.make_async_copy(t_q.at[u], f_q.at[u], fq_sem).start()
 
-    def pass_k(r, carry):
-        there = (2 * lax.rem(z + r, NZ) + c, u)
-        remote(r_kv.at[:, r], f_kv.at[z], p2k_send, fkv_sem, there).start()
+    def pass_k(h, carry):
+        @pl.when(h != z)
+        def _():
+            remote(r_kv.at[:, h], f_kv.at[z], p2k_send, fkv_sem, (2 * h + c, u)).start()
+
+        @pl.when(h == z)
+        def _():
+            pltpu.make_async_copy(r_kv.at[:, h], f_kv.at[z], fkv_sem).start()
+
         return carry
 
-    arrived(r_kv, rkv_sem)
-    lax.fori_loop(1, NZ, pass_k, 0)
-    pltpu.make_async_copy(r_kv.at[:, 0], f_kv.at[z], fkv_sem).start()
-
-    @pl.when(is_host)
-    def _():
-        arrived(dq_in.at[pl.ds(0, 15)], p1q_send)
-        arrived(kv_out.at[pl.ds(0, 31)], p1k_send)
+    for part in range(2):
+        arrived(r_kv.at[:, pl.ds(4 * part, 4)], rkv_sem.at[part])
+        lax.fori_loop(4 * part, 4 * part + 4, pass_k, 0)
+
+    @pl.when(is_host)
+    def _():
+        arrived(dq_in.at[pl.ds(0, NZ - 1)], p1q_send)
+        arrived(kv_out.at[pl.ds(0, NU - 1)], p1k_send)
 
     arrived(r_kv.at[:, pl.ds(0, NZ - 1)], p2k_send)
     arrived(t_q.at[pl.ds(0, NU - 1)], p2q_send)
@@ -457,7 +517,7 @@
         scratch_shapes=[
             pltpu.VMEM((16, 16, H), jnp.int32),
             pltpu.VMEM((3, 3, 128, 128), BF16),
-            dma, dma, dma, dma, dma((3, 3)), dma((3, 3)),
+            dma, dma((NZ,)), dma((NZ,)), dma, dma, dma, dma, dma, dma((3, 3)), dma((3, 3)),
         ],
         compiler_params=pltpu.CompilerParams(
             collective_id=0, has_side_effects=True, vmem_limit_bytes=16 * 1024 * 1024
@@ -466,13 +526,14 @@
     dq, acc = pl.pallas_call(
         gradients,
         out_shape=(
-            shape((16, 128, 128), BF16),
+            shape((NZ, 128, 128), BF16),
             shape((16, 2, 128, 128), F32),
         ),
         in_specs=[vmem, vmem, anywhere],
         out_specs=(vmem, vmem),
         scratch_shapes=[
             pltpu.SMEM((16, 128), jnp.int32),
+            pltpu.SMEM((most,), jnp.int32),
             pltpu.SMEM((most,), jnp.int32),
             pltpu.SMEM((most,), jnp.int32),
             pltpu.VMEM((most, 128 * SLOTS, 128), F32),
@@ -492,11 +553,12 @@
         in_specs=[vmem] * 2,
         out_specs=(vmem, vmem),
         scratch_shapes=[
-            pltpu.VMEM((2 * NU, NZ, 16, 128), BF16),
+            pltpu.VMEM((NU, NZ, 16, 128), BF16),
             pltpu.VMEM((3, 128, 128), BF16),
             pltpu.VMEM((6, NZ, 16, 128), BF16),
             pltpu.VMEM((NU, 32, 128), BF16),
-            dma, dma, dma, dma, dma, dma, dma, dma,
+            dma, dma, dma, dma((2,)), dma, dma, dma, dma,
+            pltpu.SemaphoreType.REGULAR,
         ],
         compiler_params=pltpu.CompilerParams(
             collective_id=1, has_side_effects=True, vmem_limit_bytes=16 * 1024 * 1024

time: 51.4 us -> 47.1 us (0.916)
  Pallas kernels: 50.7 us -> 46 us
    pallas_call x1, Pallas kernels: 28.9 us -> 15.2 us  [local(): pl.pallas_call(give_back, out_shape=(shape((NU, 32, 128), BF16), shape((N...]
    pallas_call x1, Pallas kernels: 0.05 us -> 4.62 us  [local(): pl.pallas_call(gradients, out_shape=(shape((NZ, 128, 128), BF16), shape((...]
    pallas_call x1, Pallas kernels: 21 us -> 25.4 us  [local(): pl.pallas_call(collect, out_shape=(shape((2, NZ, 2, 128, 128), BF16), sha...]
where the time goes in v3:
time: 47.1 us; the launch traced here: 46.7 us
  Pallas kernels  46 us (98%)
  between operations  0.66 us (1%)
    pallas_call x1, Pallas kernels, local(): pl.pallas_call(collect, out_shape=(shape((2, NZ, 2, 128, 128), BF16), sha...  25.4 us
    pallas_call x1, Pallas kernels, local(): pl.pallas_call(give_back, out_shape=(shape((NU, 32, 128), BF16), shape((N...  15.2 us
    pallas_call x1, Pallas kernels, local(): pl.pallas_call(gradients, out_shape=(shape((NZ, 128, 128), BF16), shape((...  4.62 us

profile of v3, /device:TPU:1, one launch (start us, length us, event | category | flops | bytes accessed | tf_op | source)
XLA Modules:
  0.0 46.7 jit_solution(11586071400674720894)
XLA Ops:
  0.6 25.4 %shard_map.85 = (bf16[2,8,2,128,128]{4,3,2,1,0:T(8,128)(2,1)S(1)}, bf16[2,8,2,128,128]{4,3,2,1,0:T(8,128)(2,1)S(1)}, s32[16,128]{1,0:T(8,128)S(1)}) custom-call(bf16[128,384]{1,0:T(8,128)(2,1)} %q_in.1, bf16[128,384]{1,0:T(8,128)(2,1)} %k_in.1, bf16[128,384]{1,0:T(8,128)(2,1)} %v_in.1, bf16[128,384]{1,0:T(8,128)(2,1)} %g_in.1, s32[16,16,48]{2,1,0:T(8,128)} %bitcast.5, ...), custom_call_target="tpu_custom_call" | custom-call | tf_op jit(solution)/shard_map/pallas_call | solution.py:508
  26.1 4.6 %shard_map.86 = (bf16[8,128,128]{2,1,0:T(8,128)(2,1)S(1)}, f32[16,2,128,128]{3,2,1,0:T(8,128)S(1)}) custom-call(bf16[16,2,128,128]{3,2,1,0:T(8,128)(2,1)S(1)} %bitcast.3, bf16[16,2,128,128]{3,2,1,0:T(8,128)(2,1)S(1)} %bitcast.4, s32[16,128]{1,0:T(8,128)S(1)} %get-tuple-element.12.picked_in), custom_call_target="tpu_custom_call" | custom-call | tf_op jit(solution)/shard_map/pallas_call | solution.py:526
  30.7 15.2 %shard_map.87 = (bf16[16,32,128]{2,1,0:T(8,128)(2,1)S(1)}, bf16[8,6,16,128]{3,2,1,0:T(8,128)(2,1)S(1)}) custom-call(bf16[8,128,128]{2,1,0:T(8,128)(2,1)S(1)} %get-tuple-element.13.dq_in, f32[16,2,128,128]{3,2,1,0:T(8,128)S(1)} %get-tuple-element.14.acc), custom_call_target="tpu_custom_call" | custom-call | tf_op jit(solution)/shard_map/pallas_call | solution.py:550
  45.9 0.8 %shard_map.88 = (bf16[8,6144]{1,0:T(8,128)(2,1)}, bf16[8,6144]{1,0:T(8,128)(2,1)}, bf16[8,6144]{1,0:T(8,128)(2,1)}) custom-call(bf16[16,32,128]{2,1,0:T(8,128)(2,1)S(1)} %get-tuple-element.15.f_q, bf16[8,6,16,128]{3,2,1,0:T(8,128)(2,1)S(1)} %get-tuple-element.16.f_kv), custom_call_target="tpu_custom_call" | custom-call | tf_op jit(solution)/shard_map/pallas_call | solution.py:568

commit v4 on v3

--- a/solution.py
+++ b/solution.py
@@ -225,7 +225,7 @@
 
 def gradients(
     kv, qg, picked_in, dq_out, acc,
-    picked, item_row, item_base, item_end, e_buf, d_buf, top_buf, row_top, row_sum, row_mix, dq_acc, sem,
+    picked, item_code, e_buf, d_buf, top_buf, row_top, row_sum, row_mix, dq_acc, sem,
 ):
     blk, u, z, c, is_host, mine = place()
 
@@ -243,15 +243,14 @@
         def listing(rows, first, end, items):
             for r in rows:
                 stop = picked[r, end]
-
-                def add(b, n, r=r, stop=stop):
-                    item_row[n] = r
-                    item_base[n] = first + b * SLOTS
-                    item_end[n] = stop
-                    return n + 1
-
-                items = lax.fori_loop(0, lax.div(stop - first + SLOTS - 1, SLOTS), add, items)
+                for base in range(first, first + NZ, SLOTS):
+                    item_code[items] = r * 4096 + base * 64 + stop
+                    items = items + (base < stop).astype(jnp.int32)
             return items
+
+        def item(i):
+            code = item_code[i]
+            return lax.shift_right_logical(code, 12), lax.bitwise_and(lax.shift_right_logical(code, 6), 63), lax.bitwise_and(code, 63)
 
         own, other = range(NZ, 16), range(NZ)
         items = listing(own, 0, COUNT, jnp.int32(0))
@@ -259,9 +258,7 @@
         needed = listing(own, SECOND, COUNT + 1, items)
         items = listing(other, SECOND, COUNT + 1, needed)
         for m in range(WIDE - 1):
-            item_row[items + m] = 0
-            item_base[items + m] = EMPTY
-            item_end[items + m] = 0
+            item_code[items + m] = EMPTY * 64
 
         def tiles(ref, r, base, part):
             return jnp.concatenate(
@@ -271,13 +268,12 @@
         def weigh(t, carry):
             for w in range(WIDE):
                 i = t * WIDE + w
-                r = item_row[i]
-                base = item_base[i]
+                r, base, end = item(i)
                 scores = nt(tiles(kv, r, base, 0), qg[r, 0]) * (FACTOR * LOG2E)
                 scores = jnp.concatenate(
                     [
                         scores[128 * m:128 * m + 128]
-                        + jnp.where(base + m < item_end[i], 0.0, -1e30)
+                        + jnp.where(base + m < end, 0.0, -1e30)
                         for m in range(SLOTS)
                     ],
                     axis=0,
@@ -304,8 +300,7 @@
         def spread(t, carry):
             for w in range(WIDE):
                 i = t * WIDE + w
-                r = item_row[i]
-                base = item_base[i]
+                r, base, _ = item(i)
                 whole = 1.0 / row_sum[r]
                 prob = e_buf[i] * (jnp.exp2(top_buf[i] - row_top[r]) * whole)
                 dscore = (prob * (d_buf[i] - row_mix[r] * whole)).astype(BF16)
@@ -393,7 +388,7 @@
                 def _():
                     remote(
                         kv_out.at[to, heights], r_kv.at[seat, heights],
-                        p1k_send, rkv_sem.at[part], (blk, to),
+                        p1k_send, rkv_sem.at[part, seat], (blk, to),
                     ).start()
 
                 return carry
@@ -420,12 +415,32 @@
         for part in range(2):
             heights = pl.ds(4 * part, 4)
             pltpu.make_async_copy(
-                kv_out.at[u, heights], r_kv.at[seat, heights], rkv_sem.at[part]
+                kv_out.at[u, heights], r_kv.at[seat, heights], rkv_sem.at[part, seat]
             ).start()
         pl.semaphore_wait(others, 2)
         send_k(0, True)
         send_q(True)
         send_k(1, True)
+
+    def pass_k(part):
+        for at in range(6):
+            arrived(r_kv.at[at, pl.ds(4 * part, 4)], rkv_sem.at[part, at])
+
+            def one(h, carry, at=at):
+                @pl.when(h != z)
+                def _():
+                    there = (2 * h + c, u)
+                    remote(r_kv.at[at, h], f_kv.at[z, at], p2k_send, fkv_sem, there).start()
+
+                @pl.when(h == z)
+                def _():
+                    pltpu.make_async_copy(r_kv.at[at, h], f_kv.at[z, at], fkv_sem).start()
+
+                return carry
+
+            lax.fori_loop(4 * part, 4 * part + 4, one, 0)
+
+    pass_k(0)
 
     arrived(r_q, rq_sem)
     heads = [r_q[l].astype(F32) for l in range(3)]
@@ -442,20 +457,7 @@
     lax.fori_loop(1, NU, pass_q, 0)
     pltpu.make_async_copy(t_q.at[u], f_q.at[u], fq_sem).start()
 
-    def pass_k(h, carry):
-        @pl.when(h != z)
-        def _():
-            remote(r_kv.at[:, h], f_kv.at[z], p2k_send, fkv_sem, (2 * h + c, u)).start()
-
-        @pl.when(h == z)
-        def _():
-            pltpu.make_async_copy(r_kv.at[:, h], f_kv.at[z], fkv_sem).start()
-
-        return carry
-
-    for part in range(2):
-        arrived(r_kv.at[:, pl.ds(4 * part, 4)], rkv_sem.at[part])
-        lax.fori_loop(4 * part, 4 * part + 4, pass_k, 0)
+    pass_k(1)
 
     @pl.when(is_host)
     def _():
@@ -534,8 +536,6 @@
         scratch_shapes=[
             pltpu.SMEM((16, 128), jnp.int32),
             pltpu.SMEM((most,), jnp.int32),
-            pltpu.SMEM((most,), jnp.int32),
-            pltpu.SMEM((most,), jnp.int32),
             pltpu.VMEM((most, 128 * SLOTS, 128), F32),
             pltpu.VMEM((most, 128 * SLOTS, 128), F32),
             pltpu.VMEM((most, 1, 128), F32),
@@ -557,7 +557,7 @@
             pltpu.VMEM((3, 128, 128), BF16),
             pltpu.VMEM((6, NZ, 16, 128), BF16),
             pltpu.VMEM((NU, 32, 128), BF16),
-            dma, dma, dma, dma((2,)), dma, dma, dma, dma,
+            dma, dma, dma, dma((2, 6)), dma, dma, dma, dma,
             pltpu.SemaphoreType.REGULAR,
         ],
         compiler_params=pltpu.CompilerParams(

time: 47.1 us -> 47.1 us (level)
  no operation moved by 1% of the time
where the time goes in v4:
time: 47.1 us; the launch traced here: 46.9 us
  Pallas kernels  46.3 us (98%)
  between operations  0.66 us (1%)
    pallas_call x1, Pallas kernels, local(): pl.pallas_call(collect, out_shape=(shape((2, NZ, 2, 128, 128), BF16), sha...  25.4 us
    pallas_call x1, Pallas kernels, local(): pl.pallas_call(give_back, out_shape=(shape((NU, 32, 128), BF16), shape((N...  15.2 us
    pallas_call x1, Pallas kernels, local(): pl.pallas_call(gradients, out_shape=(shape((NZ, 128, 128), BF16), shape((...  4.91 us

profile of v4, /device:TPU:1, one launch (start us, length us, event | category | flops | bytes accessed | tf_op | source)
XLA Modules:
  0.0 46.9 jit_solution(16615470199883385010)
XLA Ops:
  0.6 25.4 %shard_map.85 = (bf16[2,8,2,128,128]{4,3,2,1,0:T(8,128)(2,1)S(1)}, bf16[2,8,2,128,128]{4,3,2,1,0:T(8,128)(2,1)S(1)}, s32[16,128]{1,0:T(8,128)S(1)}) custom-call(bf16[128,384]{1,0:T(8,128)(2,1)} %q_in.1, bf16[128,384]{1,0:T(8,128)(2,1)} %k_in.1, bf16[128,384]{1,0:T(8,128)(2,1)} %v_in.1, bf16[128,384]{1,0:T(8,128)(2,1)} %g_in.1, s32[16,16,48]{2,1,0:T(8,128)} %bitcast.5, ...), custom_call_target="tpu_custom_call" | custom-call | tf_op jit(solution)/shard_map/pallas_call | solution.py:510
  26.1 4.9 %shard_map.86 = (bf16[8,128,128]{2,1,0:T(8,128)(2,1)S(1)}, f32[16,2,128,128]{3,2,1,0:T(8,128)S(1)}) custom-call(bf16[16,2,128,128]{3,2,1,0:T(8,128)(2,1)S(1)} %bitcast.3, bf16[16,2,128,128]{3,2,1,0:T(8,128)(2,1)S(1)} %bitcast.4, s32[16,128]{1,0:T(8,128)S(1)} %get-tuple-element.12.picked_in), custom_call_target="tpu_custom_call" | custom-call | tf_op jit(solution)/shard_map/pallas_call | solution.py:528
  31.0 15.2 %shard_map.87 = (bf16[16,32,128]{2,1,0:T(8,128)(2,1)S(1)}, bf16[8,6,16,128]{3,2,1,0:T(8,128)(2,1)S(1)}) custom-call(bf16[8,128,128]{2,1,0:T(8,128)(2,1)S(1)} %get-tuple-element.13.dq_in, f32[16,2,128,128]{3,2,1,0:T(8,128)S(1)} %get-tuple-element.14.acc), custom_call_target="tpu_custom_call" | custom-call | tf_op jit(solution)/shard_map/pallas_call | solution.py:550
  46.2 0.8 %shard_map.88 = (bf16[8,6144]{1,0:T(8,128)(2,1)}, bf16[8,6144]{1,0:T(8,128)(2,1)}, bf16[8,6144]{1,0:T(8,128)(2,1)}) custom-call(bf16[16,32,128]{2,1,0:T(8,128)(2,1)S(1)} %get-tuple-element.15.f_q, bf16[8,6,16,128]{3,2,1,0:T(8,128)(2,1)S(1)} %get-tuple-element.16.f_kv), custom_call_target="tpu_custom_call" | custom-call | tf_op jit(solution)/shard_map/pallas_call | solution.py:568

commit v5 on v3

--- a/solution.py
+++ b/solution.py
@@ -225,7 +225,7 @@
 
 def gradients(
     kv, qg, picked_in, dq_out, acc,
-    picked, item_row, item_base, item_end, e_buf, d_buf, top_buf, row_top, row_sum, row_mix, dq_acc, sem,
+    picked, item_code, e_buf, d_buf, top_buf, row_top, row_sum, row_mix, dq_acc, sem,
 ):
     blk, u, z, c, is_host, mine = place()
 
@@ -243,15 +243,14 @@
         def listing(rows, first, end, items):
             for r in rows:
                 stop = picked[r, end]
-
-                def add(b, n, r=r, stop=stop):
-                    item_row[n] = r
-                    item_base[n] = first + b * SLOTS
-                    item_end[n] = stop
-                    return n + 1
-
-                items = lax.fori_loop(0, lax.div(stop - first + SLOTS - 1, SLOTS), add, items)
+                for base in range(first, first + NZ, SLOTS):
+                    item_code[items] = r * 4096 + base * 64 + stop
+                    items = items + (base < stop).astype(jnp.int32)
             return items
+
+        def item(i):
+            code = item_code[i]
+            return lax.shift_right_logical(code, 12), lax.bitwise_and(lax.shift_right_logical(code, 6), 63), lax.bitwise_and(code, 63)
 
         own, other = range(NZ, 16), range(NZ)
         items = listing(own, 0, COUNT, jnp.int32(0))
@@ -259,32 +258,43 @@
         needed = listing(own, SECOND, COUNT + 1, items)
         items = listing(other, SECOND, COUNT + 1, needed)
         for m in range(WIDE - 1):
-            item_row[items + m] = 0
-            item_base[items + m] = EMPTY
-            item_end[items + m] = 0
-
-        def tiles(ref, r, base, part):
+            item_code[items + m] = EMPTY * 64
+
+        def keys(r, base):
+            return jnp.concatenate([kv[picked[r, base + m], 0] for m in range(SLOTS)], axis=0)
+
+        def values(r, base):
+            return jnp.concatenate([kv[picked[r, base + m], 1] for m in range(SLOTS)], axis=0)
+
+        def diagonal(r):
+            none = jnp.zeros((128, 128), BF16)
             return jnp.concatenate(
-                [ref[picked[r, base + m], part] for m in range(SLOTS)], axis=0
+                [
+                    jnp.concatenate([qg[r, 0], none], axis=1),
+                    jnp.concatenate([none, qg[r, 1]], axis=1),
+                ],
+                axis=0,
             )
 
         def weigh(t, carry):
             for w in range(WIDE):
                 i = t * WIDE + w
-                r = item_row[i]
-                base = item_base[i]
-                scores = nt(tiles(kv, r, base, 0), qg[r, 0]) * (FACTOR * LOG2E)
+                r, base, end = item(i)
+                both = nt(
+                    jnp.concatenate([keys(r, base), values(r, base)], axis=1), diagonal(r)
+                )
+                scores = both[:, :128] * (FACTOR * LOG2E)
                 scores = jnp.concatenate(
                     [
                         scores[128 * m:128 * m + 128]
-                        + jnp.where(base + m < item_end[i], 0.0, -1e30)
+                        + jnp.where(base + m < end, 0.0, -1e30)
                         for m in range(SLOTS)
                     ],
                     axis=0,
                 )
                 top = jnp.max(scores, axis=0, keepdims=True)
                 e = jnp.exp2(scores - top)
-                dprob = nt(tiles(kv, r, base, 1), qg[r, 1])
+                dprob = both[:, 128:]
                 e_buf[i] = e
                 d_buf[i] = dprob
                 top_buf[i] = top
@@ -304,21 +314,21 @@
         def spread(t, carry):
             for w in range(WIDE):
                 i = t * WIDE + w
-                r = item_row[i]
-                base = item_base[i]
+                r, base, _ = item(i)
                 whole = 1.0 / row_sum[r]
                 prob = e_buf[i] * (jnp.exp2(top_buf[i] - row_top[r]) * whole)
                 dscore = (prob * (d_buf[i] - row_mix[r] * whole)).astype(BF16)
-                dk = nn(dscore, qg[r, 0])
-                dv = nn(prob.astype(BF16), qg[r, 1])
+                both = nn(
+                    jnp.concatenate([dscore, prob.astype(BF16)], axis=1), diagonal(r)
+                )
                 dq_acc[r] += lax.dot_general(
-                    dscore, tiles(kv, r, base, 0), (((0,), (0,)), ((), ())),
+                    dscore, keys(r, base), (((0,), (0,)), ((), ())),
                     preferred_element_type=F32,
                 )
                 for m in range(SLOTS):
                     j = picked[r, base + m]
-                    acc[j, 0] += dk[128 * m:128 * m + 128]
-                    acc[j, 1] += dv[128 * m:128 * m + 128]
+                    acc[j, 0] += both[128 * m:128 * m + 128, :128]
+                    acc[j, 1] += both[128 * m:128 * m + 128, 128:]
             return carry
 
         lax.fori_loop(0, lax.div(needed + WIDE - 1, WIDE), spread, 0)
@@ -351,18 +361,6 @@
 
     lax.fori_loop(1, NZ, greet_line, 0)
     lax.fori_loop(1, NU, greet_plane, 0)
-
-    @pl.when(is_host)
-    def _():
-        def stage(r, carry):
-            dk = acc[NZ + r, 0] * FACTOR
-            dv = acc[NZ + r, 1]
-            for n in range(NU):
-                piece = jnp.concatenate([dk[8 * n:8 * n + 8], dv[8 * n:8 * n + 8]], axis=0)
-                kv_out[n, lax.rem(z + r, NZ)] = piece.astype(BF16)
-            return carry
-
-        lax.fori_loop(0, NZ, stage, 0)
 
     pl.semaphore_wait(barrier, 22 - 7 * is_host.astype(jnp.int32))
 
@@ -383,6 +381,15 @@
 
     @pl.when(is_host)
     def _():
+        def stage(h, carry):
+            r = lax.rem(h - z + NZ, NZ)
+            dk = acc[NZ + r, 0] * FACTOR
+            dv = acc[NZ + r, 1]
+            for n in range(NU):
+                piece = jnp.concatenate([dk[8 * n:8 * n + 8], dv[8 * n:8 * n + 8]], axis=0)
+                kv_out[n, h] = piece.astype(BF16)
+            return carry
+
         def send_k(part, to_hosts):
             heights = pl.ds(4 * part, 4)
 
@@ -413,18 +420,18 @@
 
             lax.fori_loop(0, NZ, one, 0)
 
-        send_k(0, False)
         send_q(False)
-        send_k(1, False)
         pltpu.make_async_copy(dq_in.at[0], r_q.at[mine], rq_sem).start()
         for part in range(2):
+            lax.fori_loop(4 * part, 4 * part + 4, stage, 0)
+            send_k(part, False)
             heights = pl.ds(4 * part, 4)
             pltpu.make_async_copy(
                 kv_out.at[u, heights], r_kv.at[seat, heights], rkv_sem.at[part]
             ).start()
         pl.semaphore_wait(others, 2)
+        send_q(True)
         send_k(0, True)
-        send_q(True)
         send_k(1, True)
 
     arrived(r_q, rq_sem)
@@ -533,8 +540,6 @@
         out_specs=(vmem, vmem),
         scratch_shapes=[
             pltpu.SMEM((16, 128), jnp.int32),
-            pltpu.SMEM((most,), jnp.int32),
-            pltpu.SMEM((most,), jnp.int32),
             pltpu.SMEM((most,), jnp.int32),
             pltpu.VMEM((most, 128 * SLOTS, 128), F32),
             pltpu.VMEM((most, 128 * SLOTS, 128), F32),

time: 47.1 us -> 47.6 us (1.011)
    pallas_call x1, Pallas kernels: 4.62 us -> 5.28 us  [local(): pl.pallas_call(gradients, out_shape=(shape((NZ, 128, 128), BF16), shape((...]
    pallas_call x1, Pallas kernels: 15.2 us -> 14.7 us  [local(): pl.pallas_call(give_back, out_shape=(shape((NU, 32, 128), BF16), shape((N...]
where the time goes in v5:
time: 47.6 us; the launch traced here: 46.8 us
  Pallas kernels  46.2 us (97%)
  between operations  0.66 us (1%)
    pallas_call x1, Pallas kernels, local(): pl.pallas_call(collect, out_shape=(shape((2, NZ, 2, 128, 128), BF16), sha...  25.4 us
    pallas_call x1, Pallas kernels, local(): pl.pallas_call(give_back, out_shape=(shape((NU, 32, 128), BF16), shape((N...  14.7 us
    pallas_call x1, Pallas kernels, local(): pl.pallas_call(gradients, out_shape=(shape((NZ, 128, 128), BF16), shape((...  5.28 us

profile of v5, /device:TPU:1, one launch (start us, length us, event | category | flops | bytes accessed | tf_op | source)
XLA Modules:
  0.0 46.8 jit_solution(14339723733549268846)
XLA Ops:
  0.6 25.4 %shard_map.85 = (bf16[2,8,2,128,128]{4,3,2,1,0:T(8,128)(2,1)S(1)}, bf16[2,8,2,128,128]{4,3,2,1,0:T(8,128)(2,1)S(1)}, s32[16,128]{1,0:T(8,128)S(1)}) custom-call(bf16[128,384]{1,0:T(8,128)(2,1)} %q_in.1, bf16[128,384]{1,0:T(8,128)(2,1)} %k_in.1, bf16[128,384]{1,0:T(8,128)(2,1)} %v_in.1, bf16[128,384]{1,0:T(8,128)(2,1)} %g_in.1, s32[16,16,48]{2,1,0:T(8,128)} %bitcast.5, ...), custom_call_target="tpu_custom_call" | custom-call | tf_op jit(solution)/shard_map/pallas_call | solution.py:515
  26.1 5.3 %shard_map.86 = (bf16[8,128,128]{2,1,0:T(8,128)(2,1)S(1)}, f32[16,2,128,128]{3,2,1,0:T(8,128)S(1)}) custom-call(bf16[16,2,128,128]{3,2,1,0:T(8,128)(2,1)S(1)} %bitcast.3, bf16[16,2,128,128]{3,2,1,0:T(8,128)(2,1)S(1)} %bitcast.4, s32[16,128]{1,0:T(8,128)S(1)} %get-tuple-element.12.picked_in), custom_call_target="tpu_custom_call" | custom-call | tf_op jit(solution)/shard_map/pallas_call | solution.py:533
  31.4 14.7 %shard_map.87 = (bf16[16,32,128]{2,1,0:T(8,128)(2,1)S(1)}, bf16[8,6,16,128]{3,2,1,0:T(8,128)(2,1)S(1)}) custom-call(bf16[8,128,128]{2,1,0:T(8,128)(2,1)S(1)} %get-tuple-element.13.dq_in, f32[16,2,128,128]{3,2,1,0:T(8,128)S(1)} %get-tuple-element.14.acc), custom_call_target="tpu_custom_call" | custom-call | tf_op jit(solution)/shard_map/pallas_call | solution.py:555
  46.1 0.8 %shard_map.88 = (bf16[8,6144]{1,0:T(8,128)(2,1)}, bf16[8,6144]{1,0:T(8,128)(2,1)}, bf16[8,6144]{1,0:T(8,128)(2,1)}) custom-call(bf16[16,32,128]{2,1,0:T(8,128)(2,1)S(1)} %get-tuple-element.15.f_q, bf16[8,6,16,128]{3,2,1,0:T(8,128)(2,1)S(1)} %get-tuple-element.16.f_kv), custom_call_target="tpu_custom_call" | custom-call | tf_op jit(solution)/shard_map/pallas_call | solution.py:573

commit v6 on v5

--- a/solution.py
+++ b/solution.py
@@ -12,8 +12,8 @@
 TILE = 128
 NZ = 8
 NU = 16
-SLOTS = 2
-WIDE = 6
+SLOTS = 1
+WIDE = 12
 SECOND = 16
 COUNT = 32
 EMPTY = 40
@@ -260,30 +260,16 @@
         for m in range(WIDE - 1):
             item_code[items + m] = EMPTY * 64
 
-        def keys(r, base):
-            return jnp.concatenate([kv[picked[r, base + m], 0] for m in range(SLOTS)], axis=0)
-
-        def values(r, base):
-            return jnp.concatenate([kv[picked[r, base + m], 1] for m in range(SLOTS)], axis=0)
-
-        def diagonal(r):
-            none = jnp.zeros((128, 128), BF16)
+        def tiles(ref, r, base, part):
             return jnp.concatenate(
-                [
-                    jnp.concatenate([qg[r, 0], none], axis=1),
-                    jnp.concatenate([none, qg[r, 1]], axis=1),
-                ],
-                axis=0,
+                [ref[picked[r, base + m], part] for m in range(SLOTS)], axis=0
             )
 
         def weigh(t, carry):
             for w in range(WIDE):
                 i = t * WIDE + w
                 r, base, end = item(i)
-                both = nt(
-                    jnp.concatenate([keys(r, base), values(r, base)], axis=1), diagonal(r)
-                )
-                scores = both[:, :128] * (FACTOR * LOG2E)
+                scores = nt(tiles(kv, r, base, 0), qg[r, 0]) * (FACTOR * LOG2E)
                 scores = jnp.concatenate(
                     [
                         scores[128 * m:128 * m + 128]
@@ -294,7 +280,7 @@
                 )
                 top = jnp.max(scores, axis=0, keepdims=True)
                 e = jnp.exp2(scores - top)
-                dprob = both[:, 128:]
+                dprob = nt(tiles(kv, r, base, 1), qg[r, 1])
                 e_buf[i] = e
                 d_buf[i] = dprob
                 top_buf[i] = top
@@ -318,17 +304,16 @@
                 whole = 1.0 / row_sum[r]
                 prob = e_buf[i] * (jnp.exp2(top_buf[i] - row_top[r]) * whole)
                 dscore = (prob * (d_buf[i] - row_mix[r] * whole)).astype(BF16)
-                both = nn(
-                    jnp.concatenate([dscore, prob.astype(BF16)], axis=1), diagonal(r)
-                )
+                dk = nn(dscore, qg[r, 0])
+                dv = nn(prob.astype(BF16), qg[r, 1])
                 dq_acc[r] += lax.dot_general(
-                    dscore, keys(r, base), (((0,), (0,)), ((), ())),
+                    dscore, tiles(kv, r, base, 0), (((0,), (0,)), ((), ())),
                     preferred_element_type=F32,
                 )
                 for m in range(SLOTS):
                     j = picked[r, base + m]
-                    acc[j, 0] += both[128 * m:128 * m + 128, :128]
-                    acc[j, 1] += both[128 * m:128 * m + 128, 128:]
+                    acc[j, 0] += dk[128 * m:128 * m + 128]
+                    acc[j, 1] += dv[128 * m:128 * m + 128]
             return carry
 
         lax.fori_loop(0, lax.div(needed + WIDE - 1, WIDE), spread, 0)

time: 47.6 us -> 47 us (0.987); the launches traced: 46.8 us -> 46.8 us
    pallas_call x1, Pallas kernels: 5.28 us -> 4.52 us  [local(): pl.pallas_call(gradients, out_shape=(shape((NZ, 128, 128), BF16), shape((...]
    pallas_call x1, Pallas kernels: 14.7 us -> 15.4 us  [local(): pl.pallas_call(give_back, out_shape=(shape((NU, 32, 128), BF16), shape((N...]
where the time goes in v6:
time: 47 us; the launch traced here: 46.8 us
  Pallas kernels  46.1 us (98%)
  between operations  0.66 us (1%)
    pallas_call x1, Pallas kernels, local(): pl.pallas_call(collect, out_shape=(shape((2, NZ, 2, 128, 128), BF16), sha...  25.4 us
    pallas_call x1, Pallas kernels, local(): pl.pallas_call(give_back, out_shape=(shape((NU, 32, 128), BF16), shape((N...  15.4 us
    pallas_call x1, Pallas kernels, local(): pl.pallas_call(gradients, out_shape=(shape((NZ, 128, 128), BF16), shape((...  4.52 us

profile of v6, /device:TPU:1, one launch (start us, length us, event | category | flops | bytes accessed | tf_op | source)
XLA Modules:
  0.0 46.8 jit_solution(7618814185451889623)
XLA Ops:
  0.6 25.4 %shard_map.85 = (bf16[2,8,2,128,128]{4,3,2,1,0:T(8,128)(2,1)S(1)}, bf16[2,8,2,128,128]{4,3,2,1,0:T(8,128)(2,1)S(1)}, s32[16,128]{1,0:T(8,128)S(1)}) custom-call(bf16[128,384]{1,0:T(8,128)(2,1)} %q_in.1, bf16[128,384]{1,0:T(8,128)(2,1)} %k_in.1, bf16[128,384]{1,0:T(8,128)(2,1)} %v_in.1, bf16[128,384]{1,0:T(8,128)(2,1)} %g_in.1, s32[16,16,48]{2,1,0:T(8,128)} %bitcast.5, ...), custom_call_target="tpu_custom_call" | custom-call | tf_op jit(solution)/shard_map/pallas_call | solution.py:500
  26.1 4.5 %shard_map.86 = (bf16[8,128,128]{2,1,0:T(8,128)(2,1)S(1)}, f32[16,2,128,128]{3,2,1,0:T(8,128)S(1)}) custom-call(bf16[16,2,128,128]{3,2,1,0:T(8,128)(2,1)S(1)} %bitcast.3, bf16[16,2,128,128]{3,2,1,0:T(8,128)(2,1)S(1)} %bitcast.4, s32[16,128]{1,0:T(8,128)S(1)} %get-tuple-element.12.picked_in), custom_call_target="tpu_custom_call" | custom-call | tf_op jit(solution)/shard_map/pallas_call | solution.py:518
  30.6 15.4 %shard_map.87 = (bf16[16,32,128]{2,1,0:T(8,128)(2,1)S(1)}, bf16[8,6,16,128]{3,2,1,0:T(8,128)(2,1)S(1)}) custom-call(bf16[8,128,128]{2,1,0:T(8,128)(2,1)S(1)} %get-tuple-element.13.dq_in, f32[16,2,128,128]{3,2,1,0:T(8,128)S(1)} %get-tuple-element.14.acc), custom_call_target="tpu_custom_call" | custom-call | tf_op jit(solution)/shard_map/pallas_call | solution.py:540
  46.0 0.8 %shard_map.88 = (bf16[8,6144]{1,0:T(8,128)(2,1)}, bf16[8,6144]{1,0:T(8,128)(2,1)}, bf16[8,6144]{1,0:T(8,128)(2,1)}) custom-call(bf16[16,32,128]{2,1,0:T(8,128)(2,1)S(1)} %get-tuple-element.15.f_q, bf16[8,6,16,128]{3,2,1,0:T(8,128)(2,1)S(1)} %get-tuple-element.16.f_kv), custom_call_target="tpu_custom_call" | custom-call | tf_op jit(solution)/shard_map/pallas_call | solution.py:558

commit v7 on v2

--- a/solution.py
+++ b/solution.py
@@ -12,9 +12,10 @@
 TILE = 128
 NZ = 8
 NU = 16
-SLOTS = 2
-WIDE = 6
+SLOTS = 1
+WIDE = 8
 COUNT = 32
+EMPTY = 40
 MESH = pl.DeviceIdType.MESH
 FACTOR = DH ** -0.5
 LOG2E = 1.4426950408889634
@@ -205,7 +206,7 @@
 
 def gradients(
     kv, qg, picked_in, dq_out, acc,
-    picked, item_row, item_base, e_buf, d_buf, top_buf, row_top, row_sum, row_mix, dq_acc, sem,
+    picked, item_code, e_buf, d_buf, top_buf, row_top, row_sum, row_mix, dq_acc, sem,
 ):
     blk, u, z, c, is_host, mine = place()
 
@@ -222,18 +223,18 @@
 
         items = jnp.int32(0)
         for r in range(16):
-            groups = lax.div(picked[r, COUNT] + SLOTS - 1, SLOTS)
-
-            def add(b, n, r=r):
-                item_row[n] = r
-                item_base[n] = b * SLOTS
-                return n + 1
-
-            items = lax.fori_loop(0, groups, add, items)
+            end = picked[r, COUNT]
+            for base in range(0, 16, SLOTS):
+                item_code[items] = r * 4096 + base * 64 + end
+                items = items + (base < end).astype(jnp.int32)
         for m in range(WIDE - 1):
-            item_row[items + m] = 0
-            item_base[items + m] = 16
+            item_code[items + m] = EMPTY * 64
         rounds = lax.div(items + WIDE - 1, WIDE)
+
+        def item(i):
+            code = item_code[i]
+            base = lax.bitwise_and(lax.shift_right_logical(code, 6), 63)
+            return lax.shift_right_logical(code, 12), base, lax.bitwise_and(code, 63)
 
         def tiles(ref, r, base, part):
             return jnp.concatenate(
@@ -243,13 +244,12 @@
         def weigh(t, carry):
             for w in range(WIDE):
                 i = t * WIDE + w
-                r = item_row[i]
-                base = item_base[i]
+                r, base, end = item(i)
                 scores = nt(tiles(kv, r, base, 0), qg[r, 0]) * (FACTOR * LOG2E)
                 scores = jnp.concatenate(
                     [
                         scores[128 * m:128 * m + 128]
-                        + jnp.where(base + m < picked[r, COUNT], 0.0, -1e30)
+                        + jnp.where(base + m < end, 0.0, -1e30)
                         for m in range(SLOTS)
                     ],
                     axis=0,
@@ -276,8 +276,7 @@
         def spread(t, carry):
             for w in range(WIDE):
                 i = t * WIDE + w
-                r = item_row[i]
-                base = item_base[i]
+                r, base, _ = item(i)
                 whole = 1.0 / row_sum[r]
                 prob = e_buf[i] * (jnp.exp2(top_buf[i] - row_top[r]) * whole)
                 dscore = (prob * (d_buf[i] - row_mix[r] * whole)).astype(BF16)
@@ -303,107 +302,148 @@
 ):
     blk, u, z, c, is_host, mine = place()
     seat = mine * 2 + lax.rem(lax.div(u, 4), 2)
+    chip_hosts = hosted(z, u)[0]
+    passes = [
+        jnp.logical_and(jnp.logical_not(is_host), jnp.logical_or(chip_hosts, c == side))
+        for side in range(2)
+    ]
     barrier = pltpu.get_barrier_semaphore()
 
+    def passer(h, line, side):
+        yes, l = hosted(h, line)
+        return 2 * h + jnp.where(yes, 1 - lax.rem(l, 2), side), line
+
     def greet(there):
-        pl.semaphore_signal(barrier, inc=1, device_id=there, device_id_type=MESH)
-
-    def greet_line(r, carry):
-        greet((2 * lax.rem(z + r, NZ) + c, u))
+        @pl.when(jnp.logical_or(there[0] != blk, there[1] != u))
+        def _():
+            pl.semaphore_signal(barrier, inc=1, device_id=there, device_id_type=MESH)
+
+    def greet_line(h, carry):
+        greet(passer(h, u, c))
         return carry
 
     def greet_plane(n, carry):
-        greet((blk, lax.rem(u + n, NU)))
+        greet(passer(z, lax.rem(u + n, NU), c))
         return carry
 
-    for l in range(3):
-        at_line = (2 * lax.rem(lift(u) + 3 * l, NZ) + l % 2, u)
-        pl.when(at_line[0] != blk)(functools.partial(greet, at_line))
-        up = lax.rem(z - 3 * l + 2 * NZ, NZ)
-        for half in range(2):
-            x = lax.div(lax.rem(up - lax.rem(up, 2) - 4 * half + NZ, NZ), 2)
-            line = 4 * (2 * lax.rem(up, 2) + half) + x
-            away = jnp.logical_or(line != u, c != l % 2)
-            pl.when(away)(functools.partial(greet, (2 * z + l % 2, line)))
-    lax.fori_loop(1, NZ, greet_line, 0)
-    lax.fori_loop(1, NU, greet_plane, 0)
+    lax.fori_loop(0, NZ, greet_line, 0)
+    lax.fori_loop(0, NU, greet_plane, 0)
+
+    @pl.when(jnp.logical_not(is_host))
+    def _():
+        for l in range(3):
+            greet((2 * lax.rem(lift(u) + 3 * l, NZ) + l % 2, u))
+            up = lax.rem(z - 3 * l + 2 * NZ, NZ)
+            for half in range(2):
+                x = lax.div(lax.rem(up - lax.rem(up, 2) - 4 * half + NZ, NZ), 2)
+                greet((2 * z + l % 2, 4 * (2 * lax.rem(up, 2) + half) + x))
+
+    alone = jnp.logical_not(chip_hosts).astype(jnp.int32)
+    pl.semaphore_wait(barrier, jnp.where(is_host, 39, 22 + 24 * (1 - alone)))
 
     @pl.when(is_host)
     def _():
-        def stage(j, carry):
-            dk = acc[j, 0] * FACTOR
-            dv = acc[j, 1]
-            for n in range(NU):
-                piece = jnp.concatenate([dk[8 * n:8 * n + 8], dv[8 * n:8 * n + 8]], axis=0)
-                kv_out[NU * lax.div(j, NZ) + n, lax.rem(j, NZ)] = piece.astype(BF16)
-            return carry
-
-        lax.fori_loop(0, 16, stage, 0)
-
-    pl.semaphore_wait(barrier, 7 + 15 + (15 + 31) * is_host.astype(jnp.int32))
+        def stage(h, carry):
+            for side in range(2):
+                j = NZ * side + lax.rem(h - z + NZ, NZ)
+                dk = acc[j, 0] * FACTOR
+                dv = acc[j, 1]
+                for n in range(NU):
+                    piece = jnp.concatenate([dk[8 * n:8 * n + 8], dv[8 * n:8 * n + 8]], axis=0)
+                    kv_out[NU * side + n, h] = piece.astype(BF16)
+            return carry
+
+        def send_q(h, carry):
+            for side in range(2):
+                tile = dq_in.at[NZ * side + lax.rem(h - z + NZ, NZ)]
+                there = passer(h, u, side)
+                remote(tile, r_q.at[side, mine], p1q_send, rq_sem.at[side], there).start()
+            return carry
+
+        lax.fori_loop(0, NZ, send_q, 0)
+        for part in range(2):
+            heights = pl.ds(4 * part, 4)
+
+            def send_k(n, carry):
+                to = lax.rem(u + n, NU)
+                for side in range(2):
+                    remote(
+                        kv_out.at[NU * side + to, heights], r_kv.at[side, seat, heights],
+                        p1k_send, rkv_sem.at[part, side], passer(z, to, side),
+                    ).start()
+                return carry
+
+            lax.fori_loop(4 * part, 4 * part + 4, stage, 0)
+            lax.fori_loop(0, NU, send_k, 0)
+
+    def pass_q(side):
+        arrived(r_q.at[side], rq_sem.at[side])
+        heads = [r_q[side, l].astype(F32) for l in range(3)]
+        for n in range(NU):
+            rows = slice(8 * n, 8 * n + 8)
+            both = jnp.concatenate([heads[0][rows], heads[1][rows]], axis=0)
+            t_q[side, n, :16] = both.astype(BF16)
+            both = jnp.concatenate([heads[2][rows], heads[2][rows]], axis=0)
+            t_q[side, n, 16:] = both.astype(BF16)
+
+        def one(n, carry):
+            to = lax.rem(u + n, NU)
+            there = (2 * z + side, to)
+            remote(t_q.at[side, to], f_q.at[u], p2q_send.at[side], fq_sem, there).start()
+            return carry
+
+        lax.fori_loop(1, NU, one, 0)
+
+        @pl.when(c != side)
+        def _():
+            one(0, 0)
+
+        @pl.when(c == side)
+        def _():
+            pltpu.make_async_copy(t_q.at[side, u], f_q.at[u], fq_sem).start()
+
+    def pass_k(part, side):
+        arrived(r_kv.at[side, :, pl.ds(4 * part, 4)], rkv_sem.at[part, side])
+
+        def one(h, carry):
+            src = r_kv.at[side, :, h]
+
+            @pl.when(jnp.logical_or(h != z, c != side))
+            def _():
+                there = (2 * h + side, u)
+                remote(src, f_kv.at[z], p2k_send.at[side], fkv_sem, there).start()
+
+            @pl.when(jnp.logical_and(h == z, c == side))
+            def _():
+                pltpu.make_async_copy(src, f_kv.at[z], fkv_sem).start()
+
+            return carry
+
+        lax.fori_loop(4 * part, 4 * part + 4, one, 0)
+
+    for side in range(2):
+        pl.when(passes[side])(functools.partial(pass_q, side))
+    for part in range(2):
+        for side in range(2):
+            pl.when(passes[side])(functools.partial(pass_k, part, side))
 
     @pl.when(is_host)
     def _():
-        for side in range(2):
-
-            def send_k(i, carry, side=side):
-                to = lax.rem(u + i, NU)
-                remote(
-                    kv_out.at[NU * side + to], r_kv.at[seat], p1k_send, rkv_sem, (2 * z + side, to)
-                ).start()
-                return carry
-
-            lax.fori_loop(1, NU, send_k, 0)
-
-            @pl.when(c != side)
-            def _():
-                send_k(0, 0)
-
-            @pl.when(c == side)
-            def _():
-                pltpu.make_async_copy(kv_out.at[NU * side + u], r_kv.at[seat], rkv_sem).start()
-
-        def send_q(n, carry):
-            there = lax.rem(blk + n, 2 * NZ)
-            r = lax.rem(lax.div(there, 2) - z + NZ, NZ)
-            tile = NZ * lax.rem(there, 2) + r
-            remote(dq_in.at[tile], r_q.at[mine], p1q_send, rq_sem, (there, u)).start()
-            return carry
-
-        lax.fori_loop(1, 2 * NZ, send_q, 0)
-        pltpu.make_async_copy(dq_in.at[NZ * c], r_q.at[mine], rq_sem).start()
-
-    arrived(r_q, rq_sem)
-    heads = [r_q[l].astype(F32) for l in range(3)]
-    for i in range(NU):
-        rows = slice(8 * i, 8 * i + 8)
-        t_q[i, :16] = jnp.concatenate([heads[0][rows], heads[1][rows]], axis=0).astype(BF16)
-        t_q[i, 16:] = jnp.concatenate([heads[2][rows], heads[2][rows]], axis=0).astype(BF16)
-
-    def pass_q(i, carry):
-        to = lax.rem(u + i, NU)
-        remote(t_q.at[to], f_q.at[u], p2q_send, fq_sem, (blk, to)).start()
-        return carry
-
-    lax.fori_loop(1, NU, pass_q, 0)
-    pltpu.make_async_copy(t_q.at[u], f_q.at[u], fq_sem).start()
-
-    def pass_k(r, carry):
-        there = (2 * lax.rem(z + r, NZ) + c, u)
-        remote(r_kv.at[:, r], f_kv.at[z], p2k_send, fkv_sem, there).start()
-        return carry
-
-    arrived(r_kv, rkv_sem)
-    lax.fori_loop(1, NZ, pass_k, 0)
-    pltpu.make_async_copy(r_kv.at[:, 0], f_kv.at[z], fkv_sem).start()
-
-    @pl.when(is_host)
-    def _():
-        arrived(dq_in.at[pl.ds(0, 15)], p1q_send)
-        arrived(kv_out.at[pl.ds(0, 31)], p1k_send)
-
-    arrived(r_kv.at[:, pl.ds(0, NZ - 1)], p2k_send)
-    arrived(t_q.at[pl.ds(0, NU - 1)], p2q_send)
+        arrived(dq_in, p1q_send)
+        arrived(kv_out, p1k_send)
+
+    for side in range(2):
+
+        @pl.when(jnp.logical_and(passes[side], c == side))
+        def _():
+            arrived(t_q.at[side, pl.ds(0, NU - 1)], p2q_send.at[side])
+            arrived(r_kv.at[side, :, pl.ds(0, NZ - 1)], p2k_send.at[side])
+
+        @pl.when(jnp.logical_and(passes[side], c != side))
+        def _():
+            arrived(t_q.at[side], p2q_send.at[side])
+            arrived(r_kv.at[side], p2k_send.at[side])
+
     arrived(f_q, fq_sem)
     arrived(f_kv, fkv_sem)
 
@@ -474,7 +514,6 @@
         scratch_shapes=[
             pltpu.SMEM((16, 128), jnp.int32),
             pltpu.SMEM((most,), jnp.int32),
-            pltpu.SMEM((most,), jnp.int32),
             pltpu.VMEM((most, 128 * SLOTS, 128), F32),
             pltpu.VMEM((most, 128 * SLOTS, 128), F32),
             pltpu.VMEM((most, 1, 128), F32),
@@ -493,10 +532,10 @@
         out_specs=(vmem, vmem),
         scratch_shapes=[
             pltpu.VMEM((2 * NU, NZ, 16, 128), BF16),
-            pltpu.VMEM((3, 128, 128), BF16),
-            pltpu.VMEM((6, NZ, 16, 128), BF16),
-            pltpu.VMEM((NU, 32, 128), BF16),
-            dma, dma, dma, dma, dma, dma, dma, dma,
+            pltpu.VMEM((2, 3, 128, 128), BF16),
+            pltpu.VMEM((2, 6, NZ, 16, 128), BF16),
+            pltpu.VMEM((2, NU, 32, 128), BF16),
+            dma, dma, dma((2,)), dma((2, 2)), dma((2,)), dma((2,)), dma, dma,
         ],
         compiler_params=pltpu.CompilerParams(
             collective_id=1, has_side_effects=True, vmem_limit_bytes=16 * 1024 * 1024

time: 51.4 us -> 48.6 us (0.946)
  Pallas kernels: 50.7 us -> 47.8 us
    pallas_call x1, Pallas kernels: 28.9 us -> 26.1 us  [local(): pl.pallas_call(give_back, out_shape=(shape((NU, 32, 128), BF16), shape((N...]
where the time goes in v7:
time: 48.6 us; the launch traced here: 48.5 us
  Pallas kernels  47.8 us (98%)
  between operations  0.66 us (1%)
    pallas_call x1, Pallas kernels, local(): pl.pallas_call(give_back, out_shape=(shape((NU, 32, 128), BF16), shape((N...  26.1 us
    pallas_call x1, Pallas kernels, local(): pl.pallas_call(collect, out_shape=(shape((2, NZ, 2, 128, 128), BF16), sha...  21 us

profile of v7, /device:TPU:1, one launch (start us, length us, event | category | flops | bytes accessed | tf_op | source)
XLA Modules:
  0.0 48.5 jit_solution(11672757411376857536)
XLA Ops:
  0.6 21.0 %shard_map.85 = (bf16[2,8,2,128,128]{4,3,2,1,0:T(8,128)(2,1)S(1)}, bf16[2,8,2,128,128]{4,3,2,1,0:T(8,128)(2,1)S(1)}, s32[16,128]{1,0:T(8,128)S(1)}) custom-call(bf16[128,384]{1,0:T(8,128)(2,1)} %q_in.1, bf16[128,384]{1,0:T(8,128)(2,1)} %k_in.1, bf16[128,384]{1,0:T(8,128)(2,1)} %v_in.1, bf16[128,384]{1,0:T(8,128)(2,1)} %g_in.1, s32[16,16,48]{2,1,0:T(8,128)} %bitcast.5, ...), custom_call_target="tpu_custom_call" | custom-call | tf_op jit(solution)/shard_map/pallas_call | solution.py:488
  21.7 26.1 %shard_map.87 = (bf16[16,32,128]{2,1,0:T(8,128)(2,1)S(1)}, bf16[8,6,16,128]{3,2,1,0:T(8,128)(2,1)S(1)}) custom-call(bf16[16,128,128]{2,1,0:T(8,128)(2,1)S(1)} %get-tuple-element.13.dq_in, f32[16,2,128,128]{3,2,1,0:T(8,128)S(1)} %get-tuple-element.14.acc), custom_call_target="tpu_custom_call" | custom-call | tf_op jit(solution)/shard_map/pallas_call | solution.py:528
  47.7 0.8 %shard_map.88 = (bf16[8,6144]{1,0:T(8,128)(2,1)}, bf16[8,6144]{1,0:T(8,128)(2,1)}, bf16[8,6144]{1,0:T(8,128)(2,1)}) custom-call(bf16[16,32,128]{2,1,0:T(8,128)(2,1)S(1)} %get-tuple-element.15.f_q, bf16[8,6,16,128]{3,2,1,0:T(8,128)(2,1)S(1)} %get-tuple-element.16.f_kv), custom_call_target="tpu_custom_call" | custom-call | tf_op jit(solution)/shard_map/pallas_call | solution.py:545
  (1 shorter events, 0.0 us)

commit v8 on v7

--- a/solution.py
+++ b/solution.py
@@ -12,8 +12,8 @@
 TILE = 128
 NZ = 8
 NU = 16
-SLOTS = 1
-WIDE = 8
+SLOTS = 2
+WIDE = 6
 COUNT = 32
 EMPTY = 40
 MESH = pl.DeviceIdType.MESH
@@ -326,11 +326,12 @@
         greet(passer(z, lax.rem(u + n, NU), c))
         return carry
 
-    lax.fori_loop(0, NZ, greet_line, 0)
-    lax.fori_loop(0, NU, greet_plane, 0)
+    greet_plane(0, 0)
 
     @pl.when(jnp.logical_not(is_host))
     def _():
+        lax.fori_loop(0, NZ, greet_line, 0)
+        lax.fori_loop(1, NU, greet_plane, 0)
         for l in range(3):
             greet((2 * lax.rem(lift(u) + 3 * l, NZ) + l % 2, u))
             up = lax.rem(z - 3 * l + 2 * NZ, NZ)
@@ -361,6 +362,8 @@
             return carry
 
         lax.fori_loop(0, NZ, send_q, 0)
+        lax.fori_loop(0, NZ, greet_line, 0)
+        lax.fori_loop(1, NU, greet_plane, 0)
         for part in range(2):
             heights = pl.ds(4 * part, 4)
 

time: 48.6 us -> 45.8 us (0.942)
  Pallas kernels: 47.8 us -> 45 us
    pallas_call x1, Pallas kernels: 26.1 us -> 23.2 us  [local(): pl.pallas_call(give_back, out_shape=(shape((NU, 32, 128), BF16), shape((N...]
where the time goes in v8:
time: 45.8 us; the launch traced here: 45.7 us
  Pallas kernels  45 us (98%)
  between operations  0.66 us (1%)
    pallas_call x1, Pallas kernels, local(): pl.pallas_call(give_back, out_shape=(shape((NU, 32, 128), BF16), shape((N...  23.2 us
    pallas_call x1, Pallas kernels, local(): pl.pallas_call(collect, out_shape=(shape((2, NZ, 2, 128, 128), BF16), sha...  21 us

profile of v8, /device:TPU:1, one launch (start us, length us, event | category | flops | bytes accessed | tf_op | source)
XLA Modules:
  0.0 45.7 jit_solution(17778554655976033766)
XLA Ops:
  0.6 21.0 %shard_map.85 = (bf16[2,8,2,128,128]{4,3,2,1,0:T(8,128)(2,1)S(1)}, bf16[2,8,2,128,128]{4,3,2,1,0:T(8,128)(2,1)S(1)}, s32[16,128]{1,0:T(8,128)S(1)}) custom-call(bf16[128,384]{1,0:T(8,128)(2,1)} %q_in.1, bf16[128,384]{1,0:T(8,128)(2,1)} %k_in.1, bf16[128,384]{1,0:T(8,128)(2,1)} %v_in.1, bf16[128,384]{1,0:T(8,128)(2,1)} %g_in.1, s32[16,16,48]{2,1,0:T(8,128)} %bitcast.5, ...), custom_call_target="tpu_custom_call" | custom-call | tf_op jit(solution)/shard_map/pallas_call | solution.py:491
  21.7 23.2 %shard_map.87 = (bf16[16,32,128]{2,1,0:T(8,128)(2,1)S(1)}, bf16[8,6,16,128]{3,2,1,0:T(8,128)(2,1)S(1)}) custom-call(bf16[16,128,128]{2,1,0:T(8,128)(2,1)S(1)} %get-tuple-element.13.dq_in, f32[16,2,128,128]{3,2,1,0:T(8,128)S(1)} %get-tuple-element.14.acc), custom_call_target="tpu_custom_call" | custom-call | tf_op jit(solution)/shard_map/pallas_call | solution.py:531
  44.9 0.8 %shard_map.88 = (bf16[8,6144]{1,0:T(8,128)(2,1)}, bf16[8,6144]{1,0:T(8,128)(2,1)}, bf16[8,6144]{1,0:T(8,128)(2,1)}) custom-call(bf16[16,32,128]{2,1,0:T(8,128)(2,1)S(1)} %get-tuple-element.15.f_q, bf16[8,6,16,128]{3,2,1,0:T(8,128)(2,1)S(1)} %get-tuple-element.16.f_kv), custom_call_target="tpu_custom_call" | custom-call | tf_op jit(solution)/shard_map/pallas_call | solution.py:548
  (1 shorter events, 0.0 us)

commit v9 on v8

--- a/solution.py
+++ b/solution.py
@@ -110,33 +110,34 @@
         )
         home = [(src.at[:, cols], dst, sem) for src, dst, sem in home]
         straight = [(src, dst, in_send, sem, there) for src, dst, sem in home]
-        around = [
+        around = straight[:1] + [
             (home[n + 1][0], passing.at[n, l], in_send, pass_sem.at[n, l], (blk, via[n]))
             for n in range(3)
-        ] + straight[:1]
+        ]
         return host, home, straight, around
 
     def nth(n, line):
         return lax.rem(z + line + n, 3)
 
-    for n in range(3):
-        l = nth(n, u)
-        host, home, straight, around = inputs(l)
-
-        @pl.when(host != z)
-        def _():
-            for move in around:
-                remote(*move).start()
-
-        @pl.when(jnp.logical_and(host == z, c != lax.rem(l, 2)))
-        def _():
-            for move in straight:
-                remote(*move).start()
-
-        @pl.when(jnp.logical_and(host == z, c == lax.rem(l, 2)))
-        def _():
-            for move in home:
-                pltpu.make_async_copy(*move).start()
+    for part in (slice(0, 1), slice(1, 4)):
+        for n in range(3):
+            l = nth(n, u)
+            host, home, straight, around = inputs(l)
+
+            @pl.when(host != z)
+            def _():
+                for move in around[part]:
+                    remote(*move).start()
+
+            @pl.when(jnp.logical_and(host == z, c != lax.rem(l, 2)))
+            def _():
+                for move in straight[part]:
+                    remote(*move).start()
+
+            @pl.when(jnp.logical_and(host == z, c == lax.rem(l, 2)))
+            def _():
+                for move in home[part]:
+                    pltpu.make_async_copy(*move).start()
 
     @pl.when(is_host)
     def _():
@@ -367,8 +368,7 @@
         for part in range(2):
             heights = pl.ds(4 * part, 4)
 
-            def send_k(n, carry):
-                to = lax.rem(u + n, NU)
+            def send_k(to, carry):
                 for side in range(2):
                     remote(
                         kv_out.at[NU * side + to, heights], r_kv.at[side, seat, heights],
@@ -389,21 +389,19 @@
             both = jnp.concatenate([heads[2][rows], heads[2][rows]], axis=0)
             t_q[side, n, 16:] = both.astype(BF16)
 
-        def one(n, carry):
-            to = lax.rem(u + n, NU)
-            there = (2 * z + side, to)
-            remote(t_q.at[side, to], f_q.at[u], p2q_send.at[side], fq_sem, there).start()
-            return carry
-
-        lax.fori_loop(1, NU, one, 0)
-
-        @pl.when(c != side)
-        def _():
-            one(0, 0)
-
-        @pl.when(c == side)
-        def _():
-            pltpu.make_async_copy(t_q.at[side, u], f_q.at[u], fq_sem).start()
+        def one(to, carry):
+            @pl.when(jnp.logical_or(to != u, c != side))
+            def _():
+                there = (2 * z + side, to)
+                remote(t_q.at[side, to], f_q.at[u], p2q_send.at[side], fq_sem, there).start()
+
+            @pl.when(jnp.logical_and(to == u, c == side))
+            def _():
+                pltpu.make_async_copy(t_q.at[side, to], f_q.at[u], fq_sem).start()
+
+            return carry
+
+        lax.fori_loop(0, NU, one, 0)
 
     def pass_k(part, side):
         arrived(r_kv.at[side, :, pl.ds(4 * part, 4)], rkv_sem.at[part, side])

time: 45.8 us -> 46.1 us (level)
  the two profiles are of different devices: /device:TPU:1 before, /device:TPU:24 now
where the time goes in v9:
time: 46.1 us; the launch traced here: 46 us
  Pallas kernels  45.4 us (98%)
  between operations  0.66 us (1%)
    pallas_call x1, Pallas kernels, local(): pl.pallas_call(give_back, out_shape=(shape((NU, 32, 128), BF16), shape((N...  25.1 us
    pallas_call x1, Pallas kernels, local(): pl.pallas_call(collect, out_shape=(shape((2, NZ, 2, 128, 128), BF16), sha...  19.5 us

profile of v9, /device:TPU:24, one launch (start us, length us, event | category | flops | bytes accessed | tf_op | source)
XLA Modules:
  0.0 46.0 jit_solution(13874715311543477769)
XLA Ops:
  0.6 19.5 %shard_map.85 = (bf16[2,8,2,128,128]{4,3,2,1,0:T(8,128)(2,1)S(1)}, bf16[2,8,2,128,128]{4,3,2,1,0:T(8,128)(2,1)S(1)}, s32[16,128]{1,0:T(8,128)S(1)}) custom-call(bf16[128,384]{1,0:T(8,128)(2,1)} %q_in.1, bf16[128,384]{1,0:T(8,128)(2,1)} %k_in.1, bf16[128,384]{1,0:T(8,128)(2,1)} %v_in.1, bf16[128,384]{1,0:T(8,128)(2,1)} %g_in.1, s32[16,16,48]{2,1,0:T(8,128)} %bitcast.5, ...), custom_call_target="tpu_custom_call" | custom-call | tf_op jit(solution)/shard_map/pallas_call | solution.py:489
  20.2 25.1 %shard_map.87 = (bf16[16,32,128]{2,1,0:T(8,128)(2,1)S(1)}, bf16[8,6,16,128]{3,2,1,0:T(8,128)(2,1)S(1)}) custom-call(bf16[16,128,128]{2,1,0:T(8,128)(2,1)S(1)} %get-tuple-element.13.dq_in, f32[16,2,128,128]{3,2,1,0:T(8,128)S(1)} %get-tuple-element.14.acc), custom_call_target="tpu_custom_call" | custom-call | tf_op jit(solution)/shard_map/pallas_call | solution.py:529
  45.3 0.8 %shard_map.88 = (bf16[8,6144]{1,0:T(8,128)(2,1)}, bf16[8,6144]{1,0:T(8,128)(2,1)}, bf16[8,6144]{1,0:T(8,128)(2,1)}) custom-call(bf16[16,32,128]{2,1,0:T(8,128)(2,1)S(1)} %get-tuple-element.15.f_q, bf16[8,6,16,128]{3,2,1,0:T(8,128)(2,1)S(1)} %get-tuple-element.16.f_kv), custom_call_target="tpu_custom_call" | custom-call | tf_op jit(solution)/shard_map/pallas_call | solution.py:546
  (1 shorter events, 0.0 us)

commit v10 on v9

--- a/solution.py
+++ b/solution.py
@@ -422,11 +422,16 @@
 
         lax.fori_loop(4 * part, 4 * part + 4, one, 0)
 
+    low = z < 2
+    for side in range(2):
+        on = jnp.logical_and(passes[side], jnp.logical_not(low))
+        pl.when(on)(functools.partial(pass_k, 0, side))
     for side in range(2):
         pl.when(passes[side])(functools.partial(pass_q, side))
-    for part in range(2):
-        for side in range(2):
-            pl.when(passes[side])(functools.partial(pass_k, part, side))
+    for side in range(2):
+        pl.when(jnp.logical_and(passes[side], low))(functools.partial(pass_k, 0, side))
+    for side in range(2):
+        pl.when(passes[side])(functools.partial(pass_k, 1, side))
 
     @pl.when(is_host)
     def _():

time: 46.1 us -> 45.6 us (0.989)
  Pallas kernels: 45.4 us -> 44.8 us
    pallas_call x1, Pallas kernels: 25.1 us -> 24.5 us  [local(): pl.pallas_call(give_back, out_shape=(shape((NU, 32, 128), BF16), shape((N...]
where the time goes in v10:
time: 45.6 us; the launch traced here: 45.5 us
  Pallas kernels  44.8 us (98%)
  between operations  0.66 us (1%)
    pallas_call x1, Pallas kernels, local(): pl.pallas_call(give_back, out_shape=(shape((NU, 32, 128), BF16), shape((N...  24.5 us
    pallas_call x1, Pallas kernels, local(): pl.pallas_call(collect, out_shape=(shape((2, NZ, 2, 128, 128), BF16), sha...  19.5 us

profile of v10, /device:TPU:24, one launch (start us, length us, event | category | flops | bytes accessed | tf_op | source)
XLA Modules:
  0.0 45.5 jit_solution(17851461236738233136)
XLA Ops:
  0.6 19.5 %shard_map.85 = (bf16[2,8,2,128,128]{4,3,2,1,0:T(8,128)(2,1)S(1)}, bf16[2,8,2,128,128]{4,3,2,1,0:T(8,128)(2,1)S(1)}, s32[16,128]{1,0:T(8,128)S(1)}) custom-call(bf16[128,384]{1,0:T(8,128)(2,1)} %q_in.1, bf16[128,384]{1,0:T(8,128)(2,1)} %k_in.1, bf16[128,384]{1,0:T(8,128)(2,1)} %v_in.1, bf16[128,384]{1,0:T(8,128)(2,1)} %g_in.1, s32[16,16,48]{2,1,0:T(8,128)} %bitcast.5, ...), custom_call_target="tpu_custom_call" | custom-call | tf_op jit(solution)/shard_map/pallas_call | solution.py:494
  20.2 24.5 %shard_map.87 = (bf16[16,32,128]{2,1,0:T(8,128)(2,1)S(1)}, bf16[8,6,16,128]{3,2,1,0:T(8,128)(2,1)S(1)}) custom-call(bf16[16,128,128]{2,1,0:T(8,128)(2,1)S(1)} %get-tuple-element.13.dq_in, f32[16,2,128,128]{3,2,1,0:T(8,128)S(1)} %get-tuple-element.14.acc), custom_call_target="tpu_custom_call" | custom-call | tf_op jit(solution)/shard_map/pallas_call | solution.py:534
  44.8 0.8 %shard_map.88 = (bf16[8,6144]{1,0:T(8,128)(2,1)}, bf16[8,6144]{1,0:T(8,128)(2,1)}, bf16[8,6144]{1,0:T(8,128)(2,1)}) custom-call(bf16[16,32,128]{2,1,0:T(8,128)(2,1)S(1)} %get-tuple-element.15.f_q, bf16[8,6,16,128]{3,2,1,0:T(8,128)(2,1)S(1)} %get-tuple-element.16.f_kv), custom_call_target="tpu_custom_call" | custom-call | tf_op jit(solution)/shard_map/pallas_call | solution.py:551
  (1 shorter events, 0.0 us)

commit v11 on v10

--- a/solution.py
+++ b/solution.py
@@ -362,11 +362,12 @@
                 remote(tile, r_q.at[side, mine], p1q_send, rq_sem.at[side], there).start()
             return carry
 
-        lax.fori_loop(0, NZ, send_q, 0)
-        lax.fori_loop(0, NZ, greet_line, 0)
-        lax.fori_loop(1, NU, greet_plane, 0)
         for part in range(2):
             heights = pl.ds(4 * part, 4)
+            lax.fori_loop(4 * part, 4 * part + 4, send_q, 0)
+            if part == 0:
+                lax.fori_loop(0, NZ, greet_line, 0)
+                lax.fori_loop(1, NU, greet_plane, 0)
 
             def send_k(to, carry):
                 for side in range(2):

time: 45.6 us -> 45.6 us (level)
  no operation moved by 1% of the time
where the time goes in v11:
time: 45.6 us; the launch traced here: 45.4 us
  Pallas kernels  44.7 us (98%)
  between operations  0.66 us (1%)
    pallas_call x1, Pallas kernels, local(): pl.pallas_call(give_back, out_shape=(shape((NU, 32, 128), BF16), shape((N...  24.4 us
    pallas_call x1, Pallas kernels, local(): pl.pallas_call(collect, out_shape=(shape((2, NZ, 2, 128, 128), BF16), sha...  19.5 us

profile of v11, /device:TPU:24, one launch (start us, length us, event | category | flops | bytes accessed | tf_op | source)
XLA Modules:
  0.0 45.4 jit_solution(10879731647295655304)
XLA Ops:
  0.6 19.5 %shard_map.85 = (bf16[2,8,2,128,128]{4,3,2,1,0:T(8,128)(2,1)S(1)}, bf16[2,8,2,128,128]{4,3,2,1,0:T(8,128)(2,1)S(1)}, s32[16,128]{1,0:T(8,128)S(1)}) custom-call(bf16[128,384]{1,0:T(8,128)(2,1)} %q_in.1, bf16[128,384]{1,0:T(8,128)(2,1)} %k_in.1, bf16[128,384]{1,0:T(8,128)(2,1)} %v_in.1, bf16[128,384]{1,0:T(8,128)(2,1)} %g_in.1, s32[16,16,48]{2,1,0:T(8,128)} %bitcast.5, ...), custom_call_target="tpu_custom_call" | custom-call | tf_op jit(solution)/shard_map/pallas_call | solution.py:495
  20.2 24.4 %shard_map.87 = (bf16[16,32,128]{2,1,0:T(8,128)(2,1)S(1)}, bf16[8,6,16,128]{3,2,1,0:T(8,128)(2,1)S(1)}) custom-call(bf16[16,128,128]{2,1,0:T(8,128)(2,1)S(1)} %get-tuple-element.13.dq_in, f32[16,2,128,128]{3,2,1,0:T(8,128)S(1)} %get-tuple-element.14.acc), custom_call_target="tpu_custom_call" | custom-call | tf_op jit(solution)/shard_map/pallas_call | solution.py:535
  44.6 0.8 %shard_map.88 = (bf16[8,6144]{1,0:T(8,128)(2,1)}, bf16[8,6144]{1,0:T(8,128)(2,1)}, bf16[8,6144]{1,0:T(8,128)(2,1)}) custom-call(bf16[16,32,128]{2,1,0:T(8,128)(2,1)S(1)} %get-tuple-element.15.f_q, bf16[8,6,16,128]{3,2,1,0:T(8,128)(2,1)S(1)} %get-tuple-element.16.f_kv), custom_call_target="tpu_custom_call" | custom-call | tf_op jit(solution)/shard_map/pallas_call | solution.py:552
  (1 shorter events, 0.0 us)

commit v12 on v11

--- a/solution.py
+++ b/solution.py
@@ -13,7 +13,7 @@
 NZ = 8
 NU = 16
 SLOTS = 2
-WIDE = 6
+WIDE = 4
 COUNT = 32
 EMPTY = 40
 MESH = pl.DeviceIdType.MESH

time: 45.6 us -> 46.6 us (1.022)
  Pallas kernels: 44.7 us -> 45.6 us
    pallas_call x1, Pallas kernels: 24.4 us -> 25.3 us  [local(): pl.pallas_call(give_back, out_shape=(shape((NU, 32, 128), BF16), shape((N...]
where the time goes in v12:
time: 46.6 us; the launch traced here: 46.3 us
  Pallas kernels  45.6 us (98%)
  between operations  0.66 us (1%)
    pallas_call x1, Pallas kernels, local(): pl.pallas_call(give_back, out_shape=(shape((NU, 32, 128), BF16), shape((N...  25.3 us
    pallas_call x1, Pallas kernels, local(): pl.pallas_call(collect, out_shape=(shape((2, NZ, 2, 128, 128), BF16), sha...  19.5 us

profile of v12, /device:TPU:24, one launch (start us, length us, event | category | flops | bytes accessed | tf_op | source)
XLA Modules:
  0.0 46.3 jit_solution(9488469519679301875)
XLA Ops:
  0.6 19.5 %shard_map.85 = (bf16[2,8,2,128,128]{4,3,2,1,0:T(8,128)(2,1)S(1)}, bf16[2,8,2,128,128]{4,3,2,1,0:T(8,128)(2,1)S(1)}, s32[16,128]{1,0:T(8,128)S(1)}) custom-call(bf16[128,384]{1,0:T(8,128)(2,1)} %q_in.1, bf16[128,384]{1,0:T(8,128)(2,1)} %k_in.1, bf16[128,384]{1,0:T(8,128)(2,1)} %v_in.1, bf16[128,384]{1,0:T(8,128)(2,1)} %g_in.1, s32[16,16,48]{2,1,0:T(8,128)} %bitcast.5, ...), custom_call_target="tpu_custom_call" | custom-call | tf_op jit(solution)/shard_map/pallas_call | solution.py:495
  20.2 25.3 %shard_map.87 = (bf16[16,32,128]{2,1,0:T(8,128)(2,1)S(1)}, bf16[8,6,16,128]{3,2,1,0:T(8,128)(2,1)S(1)}) custom-call(bf16[16,128,128]{2,1,0:T(8,128)(2,1)S(1)} %get-tuple-element.13.dq_in, f32[16,2,128,128]{3,2,1,0:T(8,128)S(1)} %get-tuple-element.14.acc), custom_call_target="tpu_custom_call" | custom-call | tf_op jit(solution)/shard_map/pallas_call | solution.py:535
  45.5 0.8 %shard_map.88 = (bf16[8,6144]{1,0:T(8,128)(2,1)}, bf16[8,6144]{1,0:T(8,128)(2,1)}, bf16[8,6144]{1,0:T(8,128)(2,1)}) custom-call(bf16[16,32,128]{2,1,0:T(8,128)(2,1)S(1)} %get-tuple-element.15.f_q, bf16[8,6,16,128]{3,2,1,0:T(8,128)(2,1)S(1)} %get-tuple-element.16.f_kv), custom_call_target="tpu_custom_call" | custom-call | tf_op jit(solution)/shard_map/pallas_call | solution.py:552
  (1 shorter events, 0.0 us)
